TPU v7x, 32 devices: a whole 2x2x4 slice. The times are simulated.
32 devices in a mesh: depth: 4 (over x, core), width: 8 (over z, y).
Axes of the slice: x: 2, y: 2, z: 4, core: 2. Of those that a mesh axis runs over, the one named last changes fastest.
Arguments:
- thermal_field: float32 [64, 256, 1024], P('depth', None, 'width'), may hold values from 1 to 3
- particulate_fraction: bfloat16 [64, 256, 1024], P('depth', None, 'width'), may hold values from 0 to 1
- sootiness_extinction: float32 [8], replicated, may hold values from 0.02 to 0.3
- vapour_extinction_rate: float32 [8], replicated, may hold values from 0.02 to 0.2
- planck_over_wavelength: float32 [8], replicated, may hold values from 2 to 8
- layer_sightline_position: int32 [4], replicated, may hold values from 0 to 3, each once
- picture_adjoint_seed: float32 [8, 256, 1024], P(None, ('depth', 'width')), may hold values from -6 to 6
Outputs:
- radiance: float32 [8, 256, 1024], P(None, ('depth', 'width'))
- temperature_gradient: float32 [64, 256, 1024], P('depth', None, 'width')
Inputs may be any that keep to these rules, and one draw needn't show every extreme that they name: `layer_sightline_position`: each slab position occurs exactly once.
All inputs are finite; a program needn't handle non-finite values.
Results may differ from a plain program's by a relative error of at most 0.0003.
Values sent between devices are 32-bit elements; how exact they have to be, the bound alone decides.
No kernel may reach another device: no remote copies, remote signals or barrier semaphores. Data moves between devices by JAX's collectives and lax.ppermute only.
A program may use at most 192 MiB of HBM per device.

v0:
```python
import functools

import jax
import jax.numpy as jnp
from jax import lax
from jax.experimental import pallas as pl
from jax.experimental.pallas import tpu as pltpu
from jax.sharding import PartitionSpec as P

LOG2E = 1.4426950408889634
ROWS = 8
FLOPS_A_US = 1e9
FAR_US, NEAR_US, PULL_US, BLEND_US = 2.4, 0.1, 4, 2.4
COPIES = 8
F32 = jnp.float32

SOOT_STEP, GAS_STEP, PLANCK_STEP, SOURCE, GAS, RATIO = range(6)
KINDS = 6


def smem():
    return pl.BlockSpec(memory_space=pltpu.SMEM)


def vmem():
    return pl.BlockSpec(memory_space=pltpu.VMEM)


def hbm():
    return pl.BlockSpec(memory_space=pltpu.HBM)


def shape(*dims):
    return jax.ShapeDtypeStruct(dims, F32)


def kernel_call(body, name, in_specs, out_specs, out_shape, us=0, mebibytes=4, scratch=()):
    def held(spec):
        return spec.memory_space == pltpu.VMEM

    def placed(spec, out):
        return pltpu.VMEM(out.shape, out.dtype) if held(spec) else out

    if isinstance(out_specs, list):
        out_shape = [placed(spec, out) for spec, out in zip(out_specs, out_shape)]
    else:
        out_shape = placed(out_specs, out_shape)
    def run(*operands, ties=()):
        def untied(*refs):
            return body(*refs[: len(in_specs)], *refs[len(in_specs) + len(ties) :])

        call = pl.pallas_call(
            untied,
            in_specs=[*in_specs, *[pl.BlockSpec(memory_space=pl.ANY)] * len(ties)],
            out_specs=out_specs,
            out_shape=out_shape,
            scratch_shapes=scratch,
            compiler_params=pltpu.CompilerParams(vmem_limit_bytes=mebibytes << 20),
            cost_estimate=pl.CostEstimate(
                flops=int(us * FLOPS_A_US), bytes_accessed=1 << 20, transcendentals=0
            ),
            name=name,
        )
        return call(
            *[
                pltpu.with_memory_space_constraint(x, pltpu.VMEM) if held(spec) else x
                for spec, x in zip(in_specs, operands)
            ],
            *ties,
        )

    return run


def rows_at(tile, count=1):
    return pl.ds(pl.multiple_of(tile * ROWS, count * ROWS), count * ROWS)


def load(soot_rate, gas_rate, planck, order, thermal, soot_share, seed, widths):
    cells, rows, columns = thermal.shape
    bands, lines, _ = seed.shape
    slabs = order.shape[0]
    half = rows // 2
    step = cells // COPIES

    def kernel(
        soot_rate_ref, gas_rate_ref, planck_ref, order_ref, thermal_hbm, soot_hbm, seed_hbm,
        thermal_ref, soot_ref, near_ref, far_ref, const_ref, *cut_refs,
    ):
        *cut_refs, sems = cut_refs
        mine = lax.axis_index("depth")
        copies = []
        for o in range(widths):
            start = pl.multiple_of((lax.axis_index("width") ^ o) * columns, columns)
            copies.append((seed_hbm.at[:, :, pl.ds(start, columns)], cut_refs[o // 2].at[o % 2]))
        for i in range(COPIES):
            part = pl.ds(i * step, step)
            copies.append((thermal_hbm.at[part], thermal_ref.at[part]))
            copies.append((soot_hbm.at[part], soot_ref.at[part]))
        copies = [pltpu.make_async_copy(a, b, sems.at[i]) for i, (a, b) in enumerate(copies)]
        for copy in copies:
            copy.start()

        def tile(value):
            return jnp.full((ROWS, columns), value, F32)

        for b in range(bands):
            gas = tile(gas_rate_ref[b]) * (1.0 / cells)
            wave = tile(planck_ref[b])
            const_ref[SOOT_STEP * bands + b] = tile(soot_rate_ref[b]) * (-LOG2E / cells)
            const_ref[GAS_STEP * bands + b] = gas * -LOG2E
            const_ref[PLANCK_STEP * bands + b] = wave * LOG2E
            const_ref[SOURCE * bands + b] = jnp.exp(wave * 0.5) - 1.0
            const_ref[GAS * bands + b] = gas
            const_ref[RATIO * bands + b] = wave / gas
        for o in range(slabs):
            front = jnp.where(order_ref[mine ^ o] < order_ref[mine], 1.0, 0.0).astype(F32)
            const_ref[KINDS * bands + o] = tile(front)
            const_ref[KINDS * bands + slabs + o] = tile(1.0 - front)
        for copy in copies:
            copy.wait()
        top = mine // (slabs // 2)
        for sums_ref, first in ((near_ref, top), (far_ref, 1 - top)):

            def add(i, _, sums_ref=sums_ref, first=first):
                here = rows_at(first * (half // ROWS) + 2 * i, 2)
                soot = soot_ref[0, here].astype(F32)
                heat = thermal_ref[0, here]
                for k in range(1, cells):
                    soot = soot + soot_ref[k, here].astype(F32)
                    heat = heat + thermal_ref[k, here]
                sums_ref[0, rows_at(2 * i, 2)] = soot
                sums_ref[1, rows_at(2 * i, 2)] = heat
                return 0

            lax.fori_loop(0, half // (2 * ROWS), add, 0)

    return kernel_call(
        kernel,
        "load",
        [smem()] * 4 + [hbm()] * 3,
        [vmem()] * (5 + widths // 2),
        [
            pltpu.VMEM(thermal.shape, thermal.dtype),
            pltpu.VMEM(soot_share.shape, soot_share.dtype),
            shape(2, half, columns),
            shape(2, half, columns),
            shape(KINDS * bands + 2 * slabs, ROWS, columns),
            *[shape(2, bands, lines, columns)] * (widths // 2),
        ],
        us=0,
        mebibytes=52,
        scratch=[pltpu.SemaphoreType.DMA((2 * COPIES + widths,))],
    )(soot_rate, gas_rate, planck, order, thermal, soot_share, seed)


def march(consts, thermal, soot_share, bands, share, o, ties, us):
    cells, _, columns = thermal.shape

    def kernel(const_ref, thermal_ref, soot_ref, part_ref, light_ref):
        first = (lax.axis_index("depth") ^ o) * share

        def tile(i, _):
            here = rows_at(first + 2 * i, 2)

            def const(kind, b):
                one = const_ref[kind * bands + b]
                return jnp.concatenate([one, one], axis=0)

            clear = [None] * bands
            light = [None] * bands
            for k in range(cells):
                heat = thermal_ref[k, here]
                soot = soot_ref[k, here].astype(F32)
                cold = pltpu.reciprocal(heat, approx=True)
                cold2 = cold * cold
                for b in range(bands):
                    fade = jnp.exp2(soot * const(SOOT_STEP, b) + heat * const(GAS_STEP, b))
                    source = pltpu.reciprocal(jnp.exp2(cold * const(PLANCK_STEP, b)) - 1.0, approx=True)
                    if k == 0:
                        beyond = fade
                        emitted = (1.0 - fade) * source
                        local = source
                    else:
                        beyond = clear[b] * fade
                        emitted = (clear[b] - beyond) * source
                        local = clear[b] * source + light[b]
                    part = (emitted + emitted * source) * (cold2 * const(RATIO, b)) + local
                    part_ref[2 * i, k, b] = part[:ROWS]
                    part_ref[2 * i + 1, k, b] = part[ROWS:]
                    light[b] = emitted if k == 0 else light[b] + emitted
                    clear[b] = beyond
            for b in range(bands):
                light_ref[2 * i, b] = light[b][:ROWS]
                light_ref[2 * i + 1, b] = light[b][ROWS:]
            return 0

        lax.fori_loop(0, share // 2, tile, 0)

    return kernel_call(
        kernel,
        "march",
        [vmem()] * 3,
        [vmem()] * 2,
        [shape(share, cells, bands, ROWS, columns), shape(share, bands, ROWS, columns)],
        us=us,
    )(consts, thermal, soot_share, ties=ties)


def turn(sources, targets, ties=()):
    arrays, names = zip(*sources)
    at = {o: (i, j) for i, held in enumerate(names) for j, o in enumerate(held)}

    def kernel(*refs):
        for target, held in zip(refs[len(arrays) :], targets):
            for j, o in enumerate(held):
                target[j] = refs[at[o][0]][at[o][1]]

    return kernel_call(
        kernel,
        "turn",
        [vmem()] * len(arrays),
        [vmem()] * len(targets),
        [shape(len(held), *arrays[0].shape[1:]) for held in targets],
    )(*arrays, ties=ties)


def join(*terms, ties=()):
    blocks, bands, lines, columns = terms[0].shape

    def kernel(*refs):
        for o in range(blocks):
            total = refs[0][o]
            for ref in refs[1 : len(terms)]:
                total = total + ref[o]
            refs[len(terms) + o % 2][o // 2] = total

    return kernel_call(
        kernel,
        "join",
        [vmem()] * len(terms),
        [vmem()] * 2,
        [shape(blocks // 2, bands, lines, columns)] * 2,
    )(*terms, ties=ties)


def dim(consts, sums, lights, slabs, twisted, ties):
    share, bands, _, columns = lights[0].shape
    half = len(lights)

    def kernel(const_ref, *refs):
        sum_refs, light_refs = refs[: slabs - 1], refs[slabs - 1 : slabs - 1 + half]
        scale_refs, seen_refs = refs[-2 * half : -half], refs[-half:]
        twist = lax.axis_index("width") if twisted else 0
        for i in range(half):

            def tile(g, _, i=i):
                here = rows_at(((lax.axis_index("depth") ^ i) & (half - 1)) * share + g)
                soot = heat = 0.0
                for j in range(1, slabs):
                    front = const_ref[KINDS * bands + j]
                    soot = soot + sum_refs[j - 1][0, here] * front
                    heat = heat + sum_refs[j - 1][1, here] * front
                for b in range(bands):
                    path = soot * const_ref[SOOT_STEP * bands + b] + heat * const_ref[GAS_STEP * bands + b]
                    scale = const_ref[SOURCE * bands + b] * jnp.exp2(path)
                    scale_refs[i][g, b] = scale
                    seen_refs[i][g ^ twist, b] = light_refs[i][g, b] * scale
                return 0

            lax.fori_loop(0, share, tile, 0)

    outs = kernel_call(
        kernel,
        "dim",
        [vmem()] * (slabs + half),
        [vmem()] * (2 * half),
        [shape(share, bands, ROWS, columns)] * (2 * half),
        us=0,
    )(consts, *sums, *lights, ties=ties)
    return outs[:half], outs[half:]


def pull(consts, seen, tangents, twisted, ties=()):
    slabs = len(seen)
    share, bands, _, columns = seen[0].shape
    half = slabs // 2

    def kernel(const_ref, *refs):
        seen_refs, tangent_refs, pull_ref = refs[:slabs], refs[slabs : 2 * slabs], refs[2 * slabs]
        twist = lax.axis_index("width") if twisted else 0
        for o in range(slabs):

            def tile(i, _, o=o):
                total = None
                for b in range(bands):
                    term = tangent_refs[o][i, b] * seen_refs[o][i, b] * const_ref[GAS * bands + b]
                    total = term if total is None else total + term
                here = rows_at(((lax.axis_index("depth") ^ o) & (half - 1)) * share + (i ^ twist))
                pull_ref[o // half, here] = total
                return 0

            lax.fori_loop(0, share, tile, 0)

    return kernel_call(
        kernel,
        "pull",
        [vmem()] * (1 + 2 * slabs),
        vmem(),
        shape(2, half * share * ROWS, columns),
        us=PULL_US,
    )(consts, *seen, *tangents, ties=ties)


def blend(consts, scales, tangents, pulls, parts, twisted, ties=()):
    slabs = len(parts)
    share, cells, bands, _, columns = parts[0].shape
    half = slabs // 2

    def kernel(const_ref, *refs):
        scale_refs, tangent_refs, pull_refs, part_refs = (
            refs[i * slabs : (i + 1) * slabs] for i in range(4)
        )
        out_hbm, token_ref, gradient_ref, sems = refs[4 * slabs :]
        token_ref[...] = jnp.zeros_like(token_ref)
        mine = lax.axis_index("depth")
        twist = lax.axis_index("width") if twisted else 0
        copies = []
        for o in range(slabs):

            def tile(g, _, o=o):
                here = rows_at(((mine ^ o) & (half - 1)) * share + g)
                weight = [
                    tangent_refs[o][g ^ twist, b] * scale_refs[o][g, b] * const_ref[GAS * bands + b]
                    for b in range(bands)
                ]
                away = None
                for j in range(slabs):
                    side = (o // half) ^ (j // half)
                    term = pull_refs[j][side, here] * const_ref[KINDS * bands + slabs + j]
                    away = term if away is None else away + term
                for k in range(cells):
                    total = part_refs[o][g, k, 0] * weight[0] - away
                    for b in range(1, bands):
                        total = total + part_refs[o][g, k, b] * weight[b]
                    gradient_ref[o, k, rows_at(g)] = total
                return 0

            lax.fori_loop(0, share, tile, 0)
            rows = rows_at((mine ^ o) * share, share)
            copies.append(pltpu.make_async_copy(gradient_ref.at[o], out_hbm.at[:, rows], sems.at[o]))
            copies[-1].start()
        for copy in copies:
            copy.wait()

    height = share * ROWS
    return kernel_call(
        kernel,
        "blend",
        [vmem()] * (1 + 4 * slabs),
        [hbm(), vmem()],
        [shape(cells, slabs * height, columns), shape(ROWS, columns)],
        us=BLEND_US,
        mebibytes=8,
        scratch=[pltpu.VMEM((slabs, cells, height, columns), F32), pltpu.SemaphoreType.DMA((slabs,))],
    )(consts, *scales, *tangents, *pulls, *parts, ties=ties)


def picture(sources, ties=()):
    arrays, names = zip(*sources)
    _, bands, lines, columns = arrays[0].shape
    count = sum(len(held) for held in names)

    def kernel(*refs):
        *block_refs, out_hbm, sems = refs
        copies = []
        for ref, held in zip(block_refs, names):
            for j, o in enumerate(held):
                start = pl.multiple_of((lax.axis_index("width") ^ o) * columns, columns)
                target = out_hbm.at[:, :, pl.ds(start, columns)]
                copies.append(pltpu.make_async_copy(ref.at[j], target, sems.at[o]))
                copies[-1].start()
        for copy in copies:
            copy.wait()

    return kernel_call(
        kernel,
        "picture",
        [vmem()] * len(arrays),
        hbm(),
        shape(bands, lines, count * columns),
        scratch=[pltpu.SemaphoreType.DMA((count,))],
    )(*arrays, ties=ties)


def solution(mesh):
    slabs = mesh.shape["depth"]
    widths = mesh.shape["width"]
    top = slabs // 2
    lower_bits = [1 << i for i in range(top.bit_length() - 1)]
    near, far = range(top), range(top, slabs)

    def swap(value, bit, axis="depth"):
        pairs = [(i, i ^ bit) for i in range(mesh.shape[axis])]
        return lax.ppermute(value, axis, pairs)

    def spread(piece, across=False):
        pieces = {top if across else 0: piece}
        for bit in reversed(lower_bits):
            for o in list(pieces):
                pieces[o ^ bit] = swap(pieces[o], bit)
        return pieces

    def lower(seen):
        kept = dict(enumerate(seen))
        for bit in lower_bits:
            for o in [o for o in kept if o & bit]:
                arrived = swap(kept.pop(o), bit)
                if bit == lower_bits[-1]:
                    return kept[0], arrived
                kept[o ^ bit] = kept[o ^ bit] + arrived

    def on_device(thermal, soot_share, soot_rate, gas_rate, planck, order, seed):
        cells, rows, columns = thermal.shape
        bands, lines, _ = seed.shape
        share = rows // slabs // ROWS
        whole = lines == ROWS

        def twist(blocks):
            at = lax.axis_index("width")
            return jnp.stack([lax.dynamic_index_in_dim(blocks, at ^ o, keepdims=False) for o in range(widths)])

        def to_tiles(blocks):
            if whole:
                return blocks
            lined = twist(blocks).transpose(1, 0, 2, 3).reshape(bands, share, ROWS, columns)
            return lined.transpose(1, 0, 2, 3)

        def to_blocks(*terms, ties=()):
            if whole:
                return join(*terms, ties=ties)
            lined = sum(terms).transpose(1, 0, 2, 3).reshape(bands, widths, lines, columns)
            blocks = twist(lined.transpose(1, 0, 2, 3))
            return blocks[0::2], blocks[1::2]

        parts, lights, scales, seen = {}, {}, {}, {}

        def lit(o, us, *ties):
            parts[o], lights[o] = march(consts, heat, soot, bands, share, o, ties, us)
            return lights[o]

        def dimmed(shares, paths, *ties):
            some = dim(
                consts, [paths[j] for j in range(1, slabs)], [lights[o] for o in shares], slabs, whole, ties
            )
            for i, o in enumerate(shares):
                scales[o], seen[o] = some[0][i], some[1][i]

        evens, odds = range(0, widths, 2), range(1, widths, 2)
        groups = [(o, o + 1) for o in evens]

        def swap_groups(arrays):
            return [arrays[0], *(swap(x, g[0], "width") for x, g in zip(arrays[1:], groups[1:]))]

        heat, soot, near_sums, far_sums, consts, *cut = load(
            soot_rate, gas_rate, planck, order, thermal, soot_share, seed, widths
        )
        across_far = swap(near_sums, top)
        across_near = swap(far_sums, top)
        cut = swap_groups(cut)
        far_paths = spread(far_sums) | spread(across_far, True)
        done = lit(far[0], FAR_US)
        even, odd = turn(list(zip(cut, groups)), [evens, odds], (done,))
        odd = swap(odd, 1, "width")
        for o in far[1:]:
            done = lit(o, FAR_US, even, done)
        dimmed(far, far_paths, done)
        (blocks,) = turn([(even, evens), (odd, odds)], [range(widths)], (seen[far[0]], across_near))
        tangent = to_tiles(blocks)
        tangents = spread(tangent)
        tangent_across = swap(tangent, top)
        near_paths = spread(near_sums) | spread(across_near, True)
        seen_far = sum(lower([seen[o] for o in far]))
        across = swap(seen_far, top)
        done = tangent
        for o in near:
            done = lit(o, NEAR_US, seen_far, done)
        (tangent_across,) = turn([(tangent_across, range(share))], [range(share)], (done,))
        dimmed(near, near_paths, tangent_across)
        tangents |= spread(tangent_across, True)
        seen_near = lower([seen[o] for o in near])
        (across,) = turn([(across, range(share))], [range(share)], (seen[near[0]],))
        pulled = pull(
            consts, [seen[o] for o in range(slabs)], [tangents[o] for o in range(slabs)], whole, (across,)
        )
        pulls = spread(pulled) | spread(swap(pulled, top), True)
        image = to_blocks(*seen_near, across, ties=(pulled,))
        image = turn([(image[0], evens), (swap(image[1], 1, "width"), odds)], groups)
        image = swap_groups(image)
        gradient, done = blend(
            consts,
            *([some[o] for o in range(slabs)] for some in (scales, tangents, pulls, parts)),
            whole,
        )
        return picture(list(zip(image, groups)), (done,)), gradient

    placed = (
        P("depth", None, "width"),
        P("depth", None, "width"),
        P(),
        P(),
        P(),
        P(),
        P(None, ("depth", "width"), None),
    )
    return jax.shard_map(
        on_device,
        mesh=mesh,
        in_specs=placed,
        out_specs=(P(None, ("depth", "width"), None), P("depth", None, "width")),
        check_vma=False,
    )
```

profile of v0, /device:TPU:0, one launch (start us, length us, event | category | flops | bytes accessed | tf_op | source)
XLA Modules:
  0.0 51.9 jit_solution(5875234619507901102)
XLA Ops:
  0.6 3.2 %load.1 = (f32[16,256,128]{2,1,0:T(8,128)S(1)}, bf16[16,256,128]{2,1,0:T(8,128)(2,1)S(1)}, f32[2,128,128]{2,1,0:T(8,128)S(1)}, f32[2,128,128]{2,1,0:T(8,128)S(1)...) custom-call(f32[8]{0:T(128)} %refs_0_.1, ...), custom_call_target="tpu_custom_call" | custom-call | bytes 1048576 | tf_op jit(solution)/shard_map/load/pallas_call | solution.py:64
  3.9 3.1 %collective-permute-start.6 = (f32[2,8,8,128]{3,2,1,0:T(8,128)S(1)}, f32[2,8,8,128]{3,2,1,0:T(8,128)S(1)}, u32[]{:S(2)}, u32[]{:S(2)}) collective-permute-start(f32[2,8,8,128]{3,2,1,0:T(8,128)S(1)} %get-tuple-element.44), channel_id=1, source_target_pairs={{0,2},{1,3},{2,0},{3,1},{4,6},{5,7},{6,4},{7,5},{8,10},{9,11},{10,... | collective-permute-start | bytes 196616 | tf_op jit(solution)/shard_map/ppermute | solution.py:405
  7.0 2.6 %collective-permute-start.7 = (f32[2,8,8,128]{3,2,1,0:T(8,128)S(1)}, f32[2,8,8,128]{3,2,1,0:T(8,128)S(1)}, u32[]{:S(2)}, u32[]{:S(2)}) collective-permute-start(f32[2,8,8,128]{3,2,1,0:T(8,128)S(1)} %get-tuple-element.45), channel_id=1, source_target_pairs={{0,4},{1,5},{2,6},{3,7},{4,0},{5,1},{6,2},{7,3},{8,12},{9,13},{10,... | collective-permute-start | bytes 196616 | tf_op jit(solution)/shard_map/ppermute | solution.py:405
  9.6 0.0 collective-permute-start.8
  9.6 1.7 %collective-permute-start.4 = (f32[2,128,128]{2,1,0:T(8,128)S(1)}, f32[2,128,128]{2,1,0:T(8,128)S(1)}, u32[]{:S(2)}, u32[]{:S(2)}) collective-permute-start(f32[2,128,128]{2,1,0:T(8,128)S(1)} %get-tuple-element.38), channel_id=1, source_target_pairs={{0,16},{8,24},{16,0},{24,8},{1,17},{9,25},{17,1},{25,9},{2,18},{10... | collective-permute-start | bytes 393224 | tf_op jit(solution)/shard_map/ppermute | solution.py:405
  11.3 0.0 collective-permute-start.3
  11.3 2.7 %march.4 = (f32[8,16,8,8,128]{4,3,2,1,0:T(8,128)S(1)}, f32[8,8,8,128]{3,2,1,0:T(8,128)S(1)}) custom-call(f32[56,8,128]{2,1,0:T(8,128)S(1)} %get-tuple-element.37.refs_0_, f32[16,256,128]{2,1,0:T(8,128)S(1)} %get-tuple-element.40.refs_1_, bf16[16,256,128]{2,1,0:T(8,128)(2,1)S(1)} %get-tuple-element.41.refs_2_), custom_call_target="tpu_custom_call" | custom-call | flops 2400000000 | bytes 1048576 | tf_op jit(solution)/shard_map/march/pallas_call | solution.py:64
  13.9 0.0 collective-permute-done.6.refs_1_
  13.9 0.4 collective-permute-start.1
  14.3 0.0 collective-permute-done.7.refs_2_
  14.3 1.3 %collective-permute-done.8.refs_3_ = f32[2,8,8,128]{3,2,1,0:T(8,128)S(1)} collective-permute-done((f32[2,8,8,128]{3,2,1,0:T(8,128)S(1)}, f32[2,8,8,128]{3,2,1,0:T(8,128)S(1)}, u32[]{:S(2)}, u32[]{:S(2)}) %collective-permute-start.8) | collective-permute-done | bytes 65568 | tf_op jit(solution)/shard_map/ppermute | solution.py:405
  15.7 1.6 %collective-permute-start.10 = (f32[4,8,8,128]{3,2,1,0:T(8,128)S(1)}, f32[4,8,8,128]{3,2,1,0:T(8,128)S(1)}, u32[]{:S(2)}, u32[]{:S(2)}) collective-permute-start(f32[4,8,8,128]{3,2,1,0:T(8,128)S(1)} %get-tuple-element.51), channel_id=1, source_target_pairs={{0,1},{1,0},{2,3},{3,2},{4,5},{5,4},{6,7},{7,6},{8,9},{9,8},{10,11... | collective-permute-start | bytes 393224 | tf_op jit(solution)/shard_map/ppermute | solution.py:405
  17.2 0.0 collective-permute-done.4.refs_2_
  17.2 0.0 collective-permute-start.5
  17.2 2.7 %march.5 = (f32[8,16,8,8,128]{4,3,2,1,0:T(8,128)S(1)}, f32[8,8,8,128]{3,2,1,0:T(8,128)S(1)}) custom-call(f32[56,8,128]{2,1,0:T(8,128)S(1)} %get-tuple-element.37.refs_0_, f32[16,256,128]{2,1,0:T(8,128)S(1)} %get-tuple-element.40.refs_1_, bf16[16,256,128]{2,1,0:T(8,128)(2,1)S(1)} %get-tuple-element.41.refs_2_, ...), custom_call_target="tpu_custom_call" | custom-call | flops 2400000000 | bytes 1048576 | tf_op jit(solution)/shard_map/march/pallas_call | solution.py:64
  19.9 0.0 collective-permute-done.5.refs_3_
  19.9 0.4 dim.2
  20.3 0.6 %collective-permute-start.9 = (f32[8,8,8,128]{3,2,1,0:T(8,128)S(1)}, f32[8,8,8,128]{3,2,1,0:T(8,128)S(1)}, u32[]{:S(2)}, u32[]{:S(2)}) collective-permute-start(f32[8,8,8,128]{3,2,1,0:T(8,128)S(1)} %get-tuple-element.50.refs_4_), channel_id=1, source_target_pairs={{0,8},{8,0},{16,24},{24,16},{1,9},{9,1},{17,25},{25,17},{2,10},{10... | collective-permute-start | bytes 786440 | tf_op jit(solution)/shard_map/ppermute | solution.py:405
  20.9 0.0 collective-permute-done.1.refs_3_.refs_2_
  20.9 1.6 %collective-permute-start.11 = (f32[8,8,8,128]{3,2,1,0:T(8,128)S(1)}, f32[8,8,8,128]{3,2,1,0:T(8,128)S(1)}, u32[]{:S(2)}, u32[]{:S(2)}) collective-permute-start(f32[8,8,8,128]{3,2,1,0:T(8,128)S(1)} %turn.6.refs_4_.refs_5_), channel_id=1, source_target_pairs={{0,16},{8,24},{16,0},{24,8},{1,17},{9,25},{17,1},{25,9},{2,18},{10... | collective-permute-start | bytes 786440 | tf_op jit(solution)/shard_map/ppermute | solution.py:405
  22.5 1.1 %collective-permute-start.13 = (f32[8,8,8,128]{3,2,1,0:T(8,128)S(1)}, f32[8,8,8,128]{3,2,1,0:T(8,128)S(1)}, u32[]{:S(2)}, u32[]{:S(2)}) collective-permute-start(f32[8,8,8,128]{3,2,1,0:T(8,128)S(1)} %add.3.refs_3_), channel_id=1, source_target_pairs={{0,16},{8,24},{16,0},{24,8},{1,17},{9,25},{17,1},{25,9},{2,18},{10... | collective-permute-start | bytes 786440 | tf_op jit(solution)/shard_map/ppermute | solution.py:405
  23.7 2.7 %march.6 = (f32[8,16,8,8,128]{4,3,2,1,0:T(8,128)S(1)}, f32[8,8,8,128]{3,2,1,0:T(8,128)S(1)}) custom-call(f32[56,8,128]{2,1,0:T(8,128)S(1)} %get-tuple-element.37.refs_0_, f32[16,256,128]{2,1,0:T(8,128)S(1)} %get-tuple-element.40.refs_1_, bf16[16,256,128]{2,1,0:T(8,128)(2,1)S(1)} %get-tuple-element.41.refs_2_, f32[8,8,8,128]{3,2,1,0:T(8,128)S(1)} %add.3.refs_3_, ...), custom_call_target="tpu_custom_call" | custom-call | flops 100000000 | bytes 1048576 | tf_op jit(solution)/shard_map/march/pallas_call | solution.py:64
  26.3 2.7 %march.7 = (f32[8,16,8,8,128]{4,3,2,1,0:T(8,128)S(1)}, f32[8,8,8,128]{3,2,1,0:T(8,128)S(1)}) custom-call(f32[56,8,128]{2,1,0:T(8,128)S(1)} %get-tuple-element.37.refs_0_, f32[16,256,128]{2,1,0:T(8,128)S(1)} %get-tuple-element.40.refs_1_, bf16[16,256,128]{2,1,0:T(8,128)(2,1)S(1)} %get-tuple-element.41.refs_2_, f32[8,8,8,128]{3,2,1,0:T(8,128)S(1)} %add.3.refs_3_, ...), custom_call_target="tpu_custom_call" | custom-call | flops 100000000 | bytes 1048576 | tf_op jit(solution)/shard_map/march/pallas_call | solution.py:64
  29.0 1.2 %collective-permute-done.11.refs_0_ = f32[8,8,8,128]{3,2,1,0:T(8,128)S(1)} collective-permute-done((f32[8,8,8,128]{3,2,1,0:T(8,128)S(1)}, f32[8,8,8,128]{3,2,1,0:T(8,128)S(1)}, u32[]{:S(2)}, u32[]{:S(2)}) %collective-permute-start.11) | collective-permute-done | bytes 262176 | tf_op jit(solution)/shard_map/ppermute | solution.py:405
  30.2 0.1 collective-permute-start.15
  30.3 0.5 collective-permute-start
  30.8 0.1 collective-permute-start.2
  30.8 1.1 %collective-permute-done.refs_1_ = f32[2,128,128]{2,1,0:T(8,128)S(1)} collective-permute-done((f32[2,128,128]{2,1,0:T(8,128)S(1)}, f32[2,128,128]{2,1,0:T(8,128)S(1)}, u32[]{:S(2)}, u32[]{:S(2)}) %collective-permute-start) | collective-permute-done | bytes 131104 | tf_op jit(solution)/shard_map/ppermute | solution.py:405
  32.0 0.2 collective-permute-done.2.refs_3_
  32.2 0.4 dim.3
  32.6 0.2 collective-permute-start.12
  32.8 2.1 %collective-permute-done.13.refs_0_ = f32[8,8,8,128]{3,2,1,0:T(8,128)S(1)} collective-permute-done((f32[8,8,8,128]{3,2,1,0:T(8,128)S(1)}, f32[8,8,8,128]{3,2,1,0:T(8,128)S(1)}, u32[]{:S(2)}, u32[]{:S(2)}) %collective-permute-start.13) | collective-permute-done | bytes 262176 | tf_op jit(solution)/shard_map/ppermute | solution.py:405
  34.9 0.0 collective-permute-done.14.refs_6_
  34.9 0.0 collective-permute-done.15.refs_8_
  34.9 0.4 pull.1.refs_3_.refs_9_
  35.3 1.6 %collective-permute-start.21 = (f32[2,128,128]{2,1,0:T(8,128)S(1)}, f32[2,128,128]{2,1,0:T(8,128)S(1)}, u32[]{:S(2)}, u32[]{:S(2)}) collective-permute-start(f32[2,128,128]{2,1,0:T(8,128)S(1)} %pull.1.refs_3_.refs_9_), channel_id=1, source_target_pairs={{0,16},{8,24},{16,0},{24,8},{1,17},{9,25},{17,1},{25,9},{2,18},{10... | collective-permute-start | bytes 393224 | tf_op jit(solution)/shard_map/ppermute | solution.py:405
  36.9 0.6 %collective-permute-start.16 = (f32[4,8,8,128]{3,2,1,0:T(8,128)S(1)}, f32[4,8,8,128]{3,2,1,0:T(8,128)S(1)}, u32[]{:S(2)}, u32[]{:S(2)}) collective-permute-start(f32[4,8,8,128]{3,2,1,0:T(8,128)S(1)} %get-tuple-element.57), channel_id=1, source_target_pairs={{0,1},{1,0},{2,3},{3,2},{4,5},{5,4},{6,7},{7,6},{8,9},{9,8},{10,11... | collective-permute-start | bytes 393224 | tf_op jit(solution)/shard_map/ppermute | solution.py:405
  37.5 0.0 collective-permute-start.20
  37.5 2.9 %collective-permute-done.21.refs_11_ = f32[2,128,128]{2,1,0:T(8,128)S(1)} collective-permute-done((f32[2,128,128]{2,1,0:T(8,128)S(1)}, f32[2,128,128]{2,1,0:T(8,128)S(1)}, u32[]{:S(2)}, u32[]{:S(2)}) %collective-permute-start.21) | collective-permute-done | bytes 131104 | tf_op jit(solution)/shard_map/ppermute | solution.py:405
  40.3 1.6 %collective-permute-done.16.refs_1_ = f32[4,8,8,128]{3,2,1,0:T(8,128)S(1)} collective-permute-done((f32[4,8,8,128]{3,2,1,0:T(8,128)S(1)}, f32[4,8,8,128]{3,2,1,0:T(8,128)S(1)}, u32[]{:S(2)}, u32[]{:S(2)}) %collective-permute-start.16) | collective-permute-done | bytes 131104 | tf_op jit(solution)/shard_map/ppermute | solution.py:405
  42.0 0.1 collective-permute-start.17
  42.0 3.1 %collective-permute-start.18 = (f32[2,8,8,128]{3,2,1,0:T(8,128)S(1)}, f32[2,8,8,128]{3,2,1,0:T(8,128)S(1)}, u32[]{:S(2)}, u32[]{:S(2)}) collective-permute-start(f32[2,8,8,128]{3,2,1,0:T(8,128)S(1)} %get-tuple-element.60), channel_id=1, source_target_pairs={{0,4},{1,5},{2,6},{3,7},{4,0},{5,1},{6,2},{7,3},{8,12},{9,13},{10,... | collective-permute-start | bytes 196616 | tf_op jit(solution)/shard_map/ppermute | solution.py:405
  45.1 1.3 %collective-permute-start.19 = (f32[2,8,8,128]{3,2,1,0:T(8,128)S(1)}, f32[2,8,8,128]{3,2,1,0:T(8,128)S(1)}, u32[]{:S(2)}, u32[]{:S(2)}) collective-permute-start(f32[2,8,8,128]{3,2,1,0:T(8,128)S(1)} %get-tuple-element.61), channel_id=1, source_target_pairs={{0,6},{1,7},{2,4},{3,5},{4,2},{5,3},{6,0},{7,1},{8,14},{9,15},{10,... | collective-permute-start | bytes 196616 | tf_op jit(solution)/shard_map/ppermute | solution.py:405
  46.4 0.0 collective-permute-done.22.refs_12_
  46.4 2.4 %blend.1 = (f32[16,256,128]{2,1,0:T(8,128)}, f32[8,128]{1,0:T(8,128)S(1)}) custom-call(f32[56,8,128]{2,1,0:T(8,128)S(1)} %get-tuple-element.37.refs_0_, f32[8,8,8,128]{3,2,1,0:T(8,128)S(1)} %get-tuple-element.62.refs_1_, f32[8,8,8,128]{3,2,1,0:T(8,128)S(1)} %get-tuple-element.63.refs_2_, f32[8,8,8,128]{3,2,1,0:T(8,128)S(1)} %get-tuple-element.64.refs_3_, ...), custom_call_target="tpu_custom_call" | custom-call | flops 2400000000 | bytes 1048576 | tf_op jit(solution)/shard_map/blend/pallas_call | solution.py:64
  48.8 0.0 collective-permute-done.18.refs_2_
  48.8 2.3 %collective-permute-done.19.refs_3_ = f32[2,8,8,128]{3,2,1,0:T(8,128)S(1)} collective-permute-done((f32[2,8,8,128]{3,2,1,0:T(8,128)S(1)}, f32[2,8,8,128]{3,2,1,0:T(8,128)S(1)}, u32[]{:S(2)}, u32[]{:S(2)}) %collective-permute-start.19) | collective-permute-done | bytes 65568 | tf_op jit(solution)/shard_map/ppermute | solution.py:405
  51.2 0.8 %picture.1 = f32[8,8,1024]{2,1,0:T(8,128)} custom-call(f32[2,8,8,128]{3,2,1,0:T(8,128)S(1)} %get-tuple-element.58.refs_0_, f32[2,8,8,128]{3,2,1,0:T(8,128)S(1)} %collective-permute-done.17.refs_1_, f32[2,8,8,128]{3,2,1,0:T(8,128)S(1)} %collective-permute-done.18.refs_2_, f32[2,8,8,128]{3,2,1,0:T(8,128)S(1)} %collective-permute-done.19.refs_3_, ...), custom_call_target="tpu_custom_call" | custom-call | bytes 1048576 | tf_op jit(solution)/shard_map/picture/pallas_call | solution.py:64
  (15 shorter events, 0.2 us)
Async XLA Ops:
  3.9 10.1 %collective-permute-start.6 = (f32[2,8,8,128]{3,2,1,0:T(8,128)S(1)}, f32[2,8,8,128]{3,2,1,0:T(8,128)S(1)}, u32[]{:S(2)}, u32[]{:S(2)}) collective-permute-start(f32[2,8,8,128]{3,2,1,0:T(8,128)S(1)} %get-tuple-element.44), channel_id=1, source_target_pairs={{0,2},{1,3},{2,0},{3,1},{4,6},{5,7},{6,4},{7,5},{8,10},{9,11},{10,... | collective-permute-start | bytes 196616 | tf_op jit(solution)/shard_map/ppermute | solution.py:405
  7.0 7.4 %collective-permute-start.7 = (f32[2,8,8,128]{3,2,1,0:T(8,128)S(1)}, f32[2,8,8,128]{3,2,1,0:T(8,128)S(1)}, u32[]{:S(2)}, u32[]{:S(2)}) collective-permute-start(f32[2,8,8,128]{3,2,1,0:T(8,128)S(1)} %get-tuple-element.45), channel_id=1, source_target_pairs={{0,4},{1,5},{2,6},{3,7},{4,0},{5,1},{6,2},{7,3},{8,12},{9,13},{10,... | collective-permute-start | bytes 196616 | tf_op jit(solution)/shard_map/ppermute | solution.py:405
  9.6 6.1 %collective-permute-start.8 = (f32[2,8,8,128]{3,2,1,0:T(8,128)S(1)}, f32[2,8,8,128]{3,2,1,0:T(8,128)S(1)}, u32[]{:S(2)}, u32[]{:S(2)}) collective-permute-start(f32[2,8,8,128]{3,2,1,0:T(8,128)S(1)} %get-tuple-element.46), channel_id=1, source_target_pairs={{0,6},{1,7},{2,4},{3,5},{4,2},{5,3},{6,0},{7,1},{8,14},{9,15},{10,... | collective-permute-start | bytes 196616 | tf_op jit(solution)/shard_map/ppermute | solution.py:405
  9.6 7.7 %collective-permute-start.4 = (f32[2,128,128]{2,1,0:T(8,128)S(1)}, f32[2,128,128]{2,1,0:T(8,128)S(1)}, u32[]{:S(2)}, u32[]{:S(2)}) collective-permute-start(f32[2,128,128]{2,1,0:T(8,128)S(1)} %get-tuple-element.38), channel_id=1, source_target_pairs={{0,16},{8,24},{16,0},{24,8},{1,17},{9,25},{17,1},{25,9},{2,18},{10... | collective-permute-start | bytes 393224 | tf_op jit(solution)/shard_map/ppermute | solution.py:405
  11.3 8.6 %collective-permute-start.3 = (f32[2,128,128]{2,1,0:T(8,128)S(1)}, f32[2,128,128]{2,1,0:T(8,128)S(1)}, u32[]{:S(2)}, u32[]{:S(2)}) collective-permute-start(f32[2,128,128]{2,1,0:T(8,128)S(1)} %get-tuple-element.39), channel_id=1, source_target_pairs={{0,8},{8,0},{16,24},{24,16},{1,9},{9,1},{17,25},{25,17},{2,10},{10... | collective-permute-start | bytes 393224 | tf_op jit(solution)/shard_map/ppermute | solution.py:405
  13.9 7.0 %collective-permute-start.1 = (f32[2,128,128]{2,1,0:T(8,128)S(1)}, f32[2,128,128]{2,1,0:T(8,128)S(1)}, u32[]{:S(2)}, u32[]{:S(2)}) collective-permute-start(f32[2,128,128]{2,1,0:T(8,128)S(1)} %get-tuple-element.39), channel_id=1, source_target_pairs={{0,16},{8,24},{16,0},{24,8},{1,17},{9,25},{17,1},{25,9},{2,18},{10... | collective-permute-start | bytes 393224 | tf_op jit(solution)/shard_map/ppermute | solution.py:405
  15.7 5.3 %collective-permute-start.10 = (f32[4,8,8,128]{3,2,1,0:T(8,128)S(1)}, f32[4,8,8,128]{3,2,1,0:T(8,128)S(1)}, u32[]{:S(2)}, u32[]{:S(2)}) collective-permute-start(f32[4,8,8,128]{3,2,1,0:T(8,128)S(1)} %get-tuple-element.51), channel_id=1, source_target_pairs={{0,1},{1,0},{2,3},{3,2},{4,5},{5,4},{6,7},{7,6},{8,9},{9,8},{10,11... | collective-permute-start | bytes 393224 | tf_op jit(solution)/shard_map/ppermute | solution.py:405
  17.2 2.7 %collective-permute-start.5 = (f32[2,128,128]{2,1,0:T(8,128)S(1)}, f32[2,128,128]{2,1,0:T(8,128)S(1)}, u32[]{:S(2)}, u32[]{:S(2)}) collective-permute-start(f32[2,128,128]{2,1,0:T(8,128)S(1)} %collective-permute-done.4.refs_2_), channel_id=1, source_target_pairs={{0,8},{8,0},{16,24},{24,16},{1,9},{9,1},{17,25},{25,17},{2,10},{10... | collective-permute-start | bytes 393224 | tf_op jit(solution)/shard_map/ppermute | solution.py:405
  20.3 2.2 %collective-permute-start.9 = (f32[8,8,8,128]{3,2,1,0:T(8,128)S(1)}, f32[8,8,8,128]{3,2,1,0:T(8,128)S(1)}, u32[]{:S(2)}, u32[]{:S(2)}) collective-permute-start(f32[8,8,8,128]{3,2,1,0:T(8,128)S(1)} %get-tuple-element.50.refs_4_), channel_id=1, source_target_pairs={{0,8},{8,0},{16,24},{24,16},{1,9},{9,1},{17,25},{25,17},{2,10},{10... | collective-permute-start | bytes 786440 | tf_op jit(solution)/shard_map/ppermute | solution.py:405
  20.9 9.2 %collective-permute-start.11 = (f32[8,8,8,128]{3,2,1,0:T(8,128)S(1)}, f32[8,8,8,128]{3,2,1,0:T(8,128)S(1)}, u32[]{:S(2)}, u32[]{:S(2)}) collective-permute-start(f32[8,8,8,128]{3,2,1,0:T(8,128)S(1)} %turn.6.refs_4_.refs_5_), channel_id=1, source_target_pairs={{0,16},{8,24},{16,0},{24,8},{1,17},{9,25},{17,1},{25,9},{2,18},{10... | collective-permute-start | bytes 786440 | tf_op jit(solution)/shard_map/ppermute | solution.py:405
  22.5 12.4 %collective-permute-start.14 = (f32[8,8,8,128]{3,2,1,0:T(8,128)S(1)}, f32[8,8,8,128]{3,2,1,0:T(8,128)S(1)}, u32[]{:S(2)}, u32[]{:S(2)}) collective-permute-start(f32[8,8,8,128]{3,2,1,0:T(8,128)S(1)} %turn.6.refs_4_.refs_5_), channel_id=1, source_target_pairs={{0,8},{8,0},{16,24},{24,16},{1,9},{9,1},{17,25},{25,17},{2,10},{10... | collective-permute-start | bytes 786440 | tf_op jit(solution)/shard_map/ppermute | solution.py:405
  22.5 12.3 %collective-permute-start.13 = (f32[8,8,8,128]{3,2,1,0:T(8,128)S(1)}, f32[8,8,8,128]{3,2,1,0:T(8,128)S(1)}, u32[]{:S(2)}, u32[]{:S(2)}) collective-permute-start(f32[8,8,8,128]{3,2,1,0:T(8,128)S(1)} %add.3.refs_3_), channel_id=1, source_target_pairs={{0,16},{8,24},{16,0},{24,8},{1,17},{9,25},{17,1},{25,9},{2,18},{10... | collective-permute-start | bytes 786440 | tf_op jit(solution)/shard_map/ppermute | solution.py:405
  30.2 4.7 %collective-permute-start.15 = (f32[8,8,8,128]{3,2,1,0:T(8,128)S(1)}, f32[8,8,8,128]{3,2,1,0:T(8,128)S(1)}, u32[]{:S(2)}, u32[]{:S(2)}) collective-permute-start(f32[8,8,8,128]{3,2,1,0:T(8,128)S(1)} %turn.7.refs_6_.refs_7_), channel_id=1, source_target_pairs={{0,8},{8,0},{16,24},{24,16},{1,9},{9,1},{17,25},{25,17},{2,10},{10... | collective-permute-start | bytes 786440 | tf_op jit(solution)/shard_map/ppermute | solution.py:405
  30.3 1.7 %collective-permute-start = (f32[2,128,128]{2,1,0:T(8,128)S(1)}, f32[2,128,128]{2,1,0:T(8,128)S(1)}, u32[]{:S(2)}, u32[]{:S(2)}) collective-permute-start(f32[2,128,128]{2,1,0:T(8,128)S(1)} %get-tuple-element.38), channel_id=1, source_target_pairs={{0,8},{8,0},{16,24},{24,16},{1,9},{9,1},{17,25},{25,17},{2,10},{10... | collective-permute-start | bytes 393224 | tf_op jit(solution)/shard_map/ppermute | solution.py:405
  30.8 1.4 %collective-permute-start.2 = (f32[2,128,128]{2,1,0:T(8,128)S(1)}, f32[2,128,128]{2,1,0:T(8,128)S(1)}, u32[]{:S(2)}, u32[]{:S(2)}) collective-permute-start(f32[2,128,128]{2,1,0:T(8,128)S(1)} %collective-permute-done.1.refs_3_.refs_2_), channel_id=1, source_target_pairs={{0,8},{8,0},{16,24},{24,16},{1,9},{9,1},{17,25},{25,17},{2,10},{10... | collective-permute-start | bytes 393224 | tf_op jit(solution)/shard_map/ppermute | solution.py:405
  32.6 4.3 %collective-permute-start.12 = (f32[8,8,8,128]{3,2,1,0:T(8,128)S(1)}, f32[8,8,8,128]{3,2,1,0:T(8,128)S(1)}, u32[]{:S(2)}, u32[]{:S(2)}) collective-permute-start(f32[8,8,8,128]{3,2,1,0:T(8,128)S(1)} %get-tuple-element.55.refs_2_), channel_id=1, source_target_pairs={{0,8},{8,0},{16,24},{24,16},{1,9},{9,1},{17,25},{25,17},{2,10},{10... | collective-permute-start | bytes 786440 | tf_op jit(solution)/shard_map/ppermute | solution.py:405
  35.3 5.0 %collective-permute-start.21 = (f32[2,128,128]{2,1,0:T(8,128)S(1)}, f32[2,128,128]{2,1,0:T(8,128)S(1)}, u32[]{:S(2)}, u32[]{:S(2)}) collective-permute-start(f32[2,128,128]{2,1,0:T(8,128)S(1)} %pull.1.refs_3_.refs_9_), channel_id=1, source_target_pairs={{0,16},{8,24},{16,0},{24,8},{1,17},{9,25},{17,1},{25,9},{2,18},{10... | collective-permute-start | bytes 393224 | tf_op jit(solution)/shard_map/ppermute | solution.py:405
  36.9 5.0 %collective-permute-start.16 = (f32[4,8,8,128]{3,2,1,0:T(8,128)S(1)}, f32[4,8,8,128]{3,2,1,0:T(8,128)S(1)}, u32[]{:S(2)}, u32[]{:S(2)}) collective-permute-start(f32[4,8,8,128]{3,2,1,0:T(8,128)S(1)} %get-tuple-element.57), channel_id=1, source_target_pairs={{0,1},{1,0},{2,3},{3,2},{4,5},{5,4},{6,7},{7,6},{8,9},{9,8},{10,11... | collective-permute-start | bytes 393224 | tf_op jit(solution)/shard_map/ppermute | solution.py:405
  37.5 8.9 %collective-permute-start.20 = (f32[2,128,128]{2,1,0:T(8,128)S(1)}, f32[2,128,128]{2,1,0:T(8,128)S(1)}, u32[]{:S(2)}, u32[]{:S(2)}) collective-permute-start(f32[2,128,128]{2,1,0:T(8,128)S(1)} %pull.1.refs_3_.refs_9_), channel_id=1, source_target_pairs={{0,8},{8,0},{16,24},{24,16},{1,9},{9,1},{17,25},{25,17},{2,10},{10... | collective-permute-start | bytes 393224 | tf_op jit(solution)/shard_map/ppermute | solution.py:405
  40.3 6.1 %collective-permute-start.22 = (f32[2,128,128]{2,1,0:T(8,128)S(1)}, f32[2,128,128]{2,1,0:T(8,128)S(1)}, u32[]{:S(2)}, u32[]{:S(2)}) collective-permute-start(f32[2,128,128]{2,1,0:T(8,128)S(1)} %collective-permute-done.21.refs_11_), channel_id=1, source_target_pairs={{0,8},{8,0},{16,24},{24,16},{1,9},{9,1},{17,25},{25,17},{2,10},{10... | collective-permute-start | bytes 393224 | tf_op jit(solution)/shard_map/ppermute | solution.py:405
  42.0 6.8 %collective-permute-start.17 = (f32[2,8,8,128]{3,2,1,0:T(8,128)S(1)}, f32[2,8,8,128]{3,2,1,0:T(8,128)S(1)}, u32[]{:S(2)}, u32[]{:S(2)}) collective-permute-start(f32[2,8,8,128]{3,2,1,0:T(8,128)S(1)} %get-tuple-element.59), channel_id=1, source_target_pairs={{0,2},{1,3},{2,0},{3,1},{4,6},{5,7},{6,4},{7,5},{8,10},{9,11},{10,... | collective-permute-start | bytes 196616 | tf_op jit(solution)/shard_map/ppermute | solution.py:405
  42.0 6.8 %collective-permute-start.18 = (f32[2,8,8,128]{3,2,1,0:T(8,128)S(1)}, f32[2,8,8,128]{3,2,1,0:T(8,128)S(1)}, u32[]{:S(2)}, u32[]{:S(2)}) collective-permute-start(f32[2,8,8,128]{3,2,1,0:T(8,128)S(1)} %get-tuple-element.60), channel_id=1, source_target_pairs={{0,4},{1,5},{2,6},{3,7},{4,0},{5,1},{6,2},{7,3},{8,12},{9,13},{10,... | collective-permute-start | bytes 196616 | tf_op jit(solution)/shard_map/ppermute | solution.py:405
  45.1 6.1 %collective-permute-start.19 = (f32[2,8,8,128]{3,2,1,0:T(8,128)S(1)}, f32[2,8,8,128]{3,2,1,0:T(8,128)S(1)}, u32[]{:S(2)}, u32[]{:S(2)}) collective-permute-start(f32[2,8,8,128]{3,2,1,0:T(8,128)S(1)} %get-tuple-element.61), channel_id=1, source_target_pairs={{0,6},{1,7},{2,4},{3,5},{4,2},{5,3},{6,0},{7,1},{8,14},{9,15},{10,... | collective-permute-start | bytes 196616 | tf_op jit(solution)/shard_map/ppermute | solution.py:405
where the time goes:
time: 52.1 us; the launch traced here: 51.9 us
  starting transfers between devices  20.1 us (39%)
  Pallas kernels  18.3 us (35%)
  waiting for transfers between devices  12.7 us (24%)
  between operations  0.8 us (2%)
    ppermute x23, starting transfers between devices, swap(): return lax.ppermute(value, axis, pairs)  20.1 us
    pallas_call x16, Pallas kernels, run(): call(*[pltpu.with_memory_space_constraint(x, pltpu.VMEM) if held(spec) el...  18.3 us
    ppermute x23, waiting for transfers between devices, swap(): return lax.ppermute(value, axis, pairs)  12.7 us
  transfers between devices with their start and end apart: 23, of which 8 were waited for; matrix products, arithmetic and copies ran while one was open for 0% of the time, Pallas kernels for 28%

commit v1 on v0

--- a/solution.py
+++ b/solution.py
@@ -10,7 +10,7 @@
 LOG2E = 1.4426950408889634
 ROWS = 8
 FLOPS_A_US = 1e9
-FAR_US, NEAR_US, PULL_US, BLEND_US = 2.4, 0.1, 4, 2.4
+FAR_US, NEAR_US, PULL_US, BLEND_US, TURN_US = 2.4, 0.1, 0, 2.4, 4
 COPIES = 8
 F32 = jnp.float32
 
@@ -207,7 +207,7 @@
     )(consts, thermal, soot_share, ties=ties)
 
 
-def turn(sources, targets, ties=()):
+def turn(sources, targets, ties=(), us=0):
     arrays, names = zip(*sources)
     at = {o: (i, j) for i, held in enumerate(names) for j, o in enumerate(held)}
 
@@ -222,6 +222,7 @@
         [vmem()] * len(arrays),
         [vmem()] * len(targets),
         [shape(len(held), *arrays[0].shape[1:]) for held in targets],
+        us=us,
     )(*arrays, ties=ties)
 
 
@@ -241,6 +242,16 @@
         [vmem()] * len(terms),
         [vmem()] * 2,
         [shape(blocks // 2, bands, lines, columns)] * 2,
+    )(*terms, ties=ties)
+
+
+def total(terms, ties):
+    def kernel(*refs):
+        for i in range(terms[0].shape[0]):
+            refs[-1][i] = sum((ref[i] for ref in refs[1:-1]), refs[0][i])
+
+    return kernel_call(
+        kernel, "total", [vmem()] * len(terms), vmem(), shape(*terms[0].shape)
     )(*terms, ties=ties)
 
 
@@ -469,33 +480,50 @@
         across_near = swap(far_sums, top)
         cut = swap_groups(cut)
         far_paths = spread(far_sums) | spread(across_far, True)
+        every, tiles = range(widths), range(share)
+        sorted_blocks = [*evens, *odds]
+
+        def side(blocks, s):
+            return [(o, s) for o in blocks]
+
+        def both(blocks):
+            return side(blocks, 0) + side(blocks, 1)
+
         done = lit(far[0], FAR_US)
-        even, odd = turn(list(zip(cut, groups)), [evens, odds], (done,))
+        (mine,) = turn(list(zip(cut, groups)), [sorted_blocks], (done,))
+        theirs = swap(mine, top)
+        for o in far[1:]:
+            done = lit(o, FAR_US, mine, done, across_near)
+        dimmed(far, far_paths, done)
+        even, odd = turn(
+            [(mine, side(sorted_blocks, 0)), (theirs, side(sorted_blocks, 1))],
+            [both(evens), both(odds)],
+            (seen[far[0]],),
+            us=TURN_US,
+        )
         odd = swap(odd, 1, "width")
-        for o in far[1:]:
-            done = lit(o, FAR_US, even, done)
-        dimmed(far, far_paths, done)
-        (blocks,) = turn([(even, evens), (odd, odds)], [range(widths)], (seen[far[0]], across_near))
-        tangent = to_tiles(blocks)
-        tangents = spread(tangent)
-        tangent_across = swap(tangent, top)
         near_paths = spread(near_sums) | spread(across_near, True)
-        seen_far = sum(lower([seen[o] for o in far]))
+        cores = [near_paths[o] for o in near_paths if o not in (0, top)]
+        seen_far = total(lower([seen[o] for o in far]), (even,))
         across = swap(seen_far, top)
-        done = tangent
+        done = seen_far
         for o in near:
-            done = lit(o, NEAR_US, seen_far, done)
-        (tangent_across,) = turn([(tangent_across, range(share))], [range(share)], (done,))
-        dimmed(near, near_paths, tangent_across)
-        tangents |= spread(tangent_across, True)
+            done = lit(o, NEAR_US, seen_far, done, *(cores if o else ()))
+        dimmed(near, near_paths, done)
         seen_near = lower([seen[o] for o in near])
-        (across,) = turn([(across, range(share))], [range(share)], (seen[near[0]],))
+        blocks = turn(
+            [(even, both(evens)), (odd, both(odds))], [side(every, 0), side(every, 1)], (seen[near[0]],)
+        )
+        tangents = spread(to_tiles(blocks[0])) | spread(to_tiles(blocks[1]), True)
+        (across,) = turn([(across, tiles)], [tiles], (blocks[0],))
+        (across,) = turn([(across, tiles)], [tiles], us=TURN_US)
+        image = to_blocks(*seen_near, across)
+        odd = swap(image[1], 1, "width")
         pulled = pull(
-            consts, [seen[o] for o in range(slabs)], [tangents[o] for o in range(slabs)], whole, (across,)
-        )
-        pulls = spread(pulled) | spread(swap(pulled, top), True)
-        image = to_blocks(*seen_near, across, ties=(pulled,))
-        image = turn([(image[0], evens), (swap(image[1], 1, "width"), odds)], groups)
+            consts, [seen[o] for o in range(slabs)], [tangents[o] for o in range(slabs)], whole, (image[0],)
+        )
+        pulls = {o: swap(pulled, o) if o else pulled for o in range(slabs)}
+        image = turn([(image[0], evens), (odd, odds)], groups, (pulled,))
         image = swap_groups(image)
         gradient, done = blend(
             consts,

time: 52.1 us -> 50.6 us (0.971)
  waiting for transfers between devices: 12.7 us -> 10.1 us
  starting transfers between devices: 20.1 us -> 21.1 us
    ppermute x23, waiting for transfers between devices: 12.7 us -> 10.1 us  [swap(): return lax.ppermute(value, axis, pairs)]
    ppermute x23, starting transfers between devices: 20.1 us -> 21.1 us  [swap(): return lax.ppermute(value, axis, pairs)]
    pallas_call x16 -> x18, Pallas kernels: 18.3 us -> 18.4 us  [run(): call(*[pltpu.with_memory_space_constraint(x, pltpu.VMEM) if held(spec) el...]
  transfers between devices with their start and end apart: 23 -> 23, of which waited for: 8 -> 8; matrix products, arithmetic and copies ran while one was open for 0% -> 0% of each run, Pallas kernels for 28% -> 29%
where the time goes in v1:
time: 50.6 us; the launch traced here: 50.4 us
  starting transfers between devices  21.1 us (42%)
  Pallas kernels  18.4 us (36%)
  waiting for transfers between devices  10.1 us (20%)
  between operations  0.81 us (2%)
    ppermute x23, starting transfers between devices, swap(): return lax.ppermute(value, axis, pairs)  21.1 us
    pallas_call x18, Pallas kernels, run(): call(*[pltpu.with_memory_space_constraint(x, pltpu.VMEM) if held(spec) el...  18.4 us
    ppermute x23, waiting for transfers between devices, swap(): return lax.ppermute(value, axis, pairs)  10.1 us
  transfers between devices with their start and end apart: 23, of which 8 were waited for; matrix products, arithmetic and copies ran while one was open for 0% of the time, Pallas kernels for 29%

profile of v1, /device:TPU:0, one launch (start us, length us, event | category | flops | bytes accessed | tf_op | source)
XLA Modules:
  0.0 50.4 jit_solution(6290583526733809783)
XLA Ops:
  0.6 3.2 %load.1 = (f32[16,256,128]{2,1,0:T(8,128)S(1)}, bf16[16,256,128]{2,1,0:T(8,128)(2,1)S(1)}, f32[2,128,128]{2,1,0:T(8,128)S(1)}, f32[2,128,128]{2,1,0:T(8,128)S(1)...) custom-call(f32[8]{0:T(128)} %refs_0_.1, ...), custom_call_target="tpu_custom_call" | custom-call | bytes 1048576 | tf_op jit(solution)/shard_map/load/pallas_call | solution.py:64
  3.9 3.1 %collective-permute-start.6 = (f32[2,8,8,128]{3,2,1,0:T(8,128)S(1)}, f32[2,8,8,128]{3,2,1,0:T(8,128)S(1)}, u32[]{:S(2)}, u32[]{:S(2)}) collective-permute-start(f32[2,8,8,128]{3,2,1,0:T(8,128)S(1)} %get-tuple-element.46), channel_id=1, source_target_pairs={{0,2},{1,3},{2,0},{3,1},{4,6},{5,7},{6,4},{7,5},{8,10},{9,11},{10,... | collective-permute-start | bytes 196616 | tf_op jit(solution)/shard_map/ppermute | solution.py:416
  7.0 2.6 %collective-permute-start.7 = (f32[2,8,8,128]{3,2,1,0:T(8,128)S(1)}, f32[2,8,8,128]{3,2,1,0:T(8,128)S(1)}, u32[]{:S(2)}, u32[]{:S(2)}) collective-permute-start(f32[2,8,8,128]{3,2,1,0:T(8,128)S(1)} %get-tuple-element.47), channel_id=1, source_target_pairs={{0,4},{1,5},{2,6},{3,7},{4,0},{5,1},{6,2},{7,3},{8,12},{9,13},{10,... | collective-permute-start | bytes 196616 | tf_op jit(solution)/shard_map/ppermute | solution.py:416
  9.6 0.0 collective-permute-start.8
  9.6 1.7 %collective-permute-start.1 = (f32[2,128,128]{2,1,0:T(8,128)S(1)}, f32[2,128,128]{2,1,0:T(8,128)S(1)}, u32[]{:S(2)}, u32[]{:S(2)}) collective-permute-start(f32[2,128,128]{2,1,0:T(8,128)S(1)} %get-tuple-element.41), channel_id=1, source_target_pairs={{0,16},{8,24},{16,0},{24,8},{1,17},{9,25},{17,1},{25,9},{2,18},{10... | collective-permute-start | bytes 393224 | tf_op jit(solution)/shard_map/ppermute | solution.py:416
  11.3 0.3 collective-permute-start.4
  11.6 2.7 %march.4 = (f32[8,16,8,8,128]{4,3,2,1,0:T(8,128)S(1)}, f32[8,8,8,128]{3,2,1,0:T(8,128)S(1)}) custom-call(f32[56,8,128]{2,1,0:T(8,128)S(1)} %get-tuple-element.39.refs_0_, f32[16,256,128]{2,1,0:T(8,128)S(1)} %get-tuple-element.42.refs_1_, bf16[16,256,128]{2,1,0:T(8,128)(2,1)S(1)} %get-tuple-element.43.refs_2_), custom_call_target="tpu_custom_call" | custom-call | flops 2400000000 | bytes 1048576 | tf_op jit(solution)/shard_map/march/pallas_call | solution.py:64
  14.3 0.0 collective-permute-done.7.refs_2_
  14.3 1.4 %collective-permute-done.8.refs_3_ = f32[2,8,8,128]{3,2,1,0:T(8,128)S(1)} collective-permute-done((f32[2,8,8,128]{3,2,1,0:T(8,128)S(1)}, f32[2,8,8,128]{3,2,1,0:T(8,128)S(1)}, u32[]{:S(2)}, u32[]{:S(2)}) %collective-permute-start.8) | collective-permute-done | bytes 65568 | tf_op jit(solution)/shard_map/ppermute | solution.py:416
  15.7 1.6 %collective-permute-start.10 = (f32[8,8,8,128]{3,2,1,0:T(8,128)S(1)}, f32[8,8,8,128]{3,2,1,0:T(8,128)S(1)}, u32[]{:S(2)}, u32[]{:S(2)}) collective-permute-start(f32[8,8,8,128]{3,2,1,0:T(8,128)S(1)} %turn.6.refs_3_.refs_0_), channel_id=1, source_target_pairs={{0,16},{8,24},{16,0},{24,8},{1,17},{9,25},{17,1},{25,9},{2,18},{10... | collective-permute-start | bytes 786440 | tf_op jit(solution)/shard_map/ppermute | solution.py:416
  17.2 0.0 collective-permute-start.3
  17.2 0.3 collective-permute-done.4.refs_2_
  17.5 0.2 collective-permute-start.5
  17.7 2.7 %march.5 = (f32[8,16,8,8,128]{4,3,2,1,0:T(8,128)S(1)}, f32[8,8,8,128]{3,2,1,0:T(8,128)S(1)}) custom-call(f32[56,8,128]{2,1,0:T(8,128)S(1)} %get-tuple-element.39.refs_0_, f32[16,256,128]{2,1,0:T(8,128)S(1)} %get-tuple-element.42.refs_1_, bf16[16,256,128]{2,1,0:T(8,128)(2,1)S(1)} %get-tuple-element.43.refs_2_, f32[8,8,8,128]{3,2,1,0:T(8,128)S(1)} %turn.6.refs_3_.refs_0_, ...), custom_call_target="tpu_custom_call" | custom-call | flops 2400000000 | bytes 1048576 | tf_op jit(solution)/shard_map/march/pallas_call | solution.py:64
  20.4 0.0 collective-permute-done.5.refs_3_
  20.4 0.4 dim.2
  20.8 0.3 collective-permute-start.9
  21.2 1.5 %collective-permute-done.10.refs_1_ = f32[8,8,8,128]{3,2,1,0:T(8,128)S(1)} collective-permute-done((f32[8,8,8,128]{3,2,1,0:T(8,128)S(1)}, f32[8,8,8,128]{3,2,1,0:T(8,128)S(1)}, u32[]{:S(2)}, u32[]{:S(2)}) %collective-permute-start.10) | collective-permute-done | bytes 262176 | tf_op jit(solution)/shard_map/ppermute | solution.py:416
  22.7 1.6 %collective-permute-start.13 = (f32[8,8,8,128]{3,2,1,0:T(8,128)S(1)}, f32[8,8,8,128]{3,2,1,0:T(8,128)S(1)}, u32[]{:S(2)}, u32[]{:S(2)}) collective-permute-start(f32[8,8,8,128]{3,2,1,0:T(8,128)S(1)} %get-tuple-element.57), channel_id=1, source_target_pairs={{0,1},{1,0},{2,3},{3,2},{4,5},{5,4},{6,7},{7,6},{8,9},{9,8},{10,11... | collective-permute-start | bytes 786440 | tf_op jit(solution)/shard_map/ppermute | solution.py:416
  24.3 0.0 collective-permute-done.9.refs_1_
  24.3 1.6 %collective-permute-start.12 = (f32[8,8,8,128]{3,2,1,0:T(8,128)S(1)}, f32[8,8,8,128]{3,2,1,0:T(8,128)S(1)}, u32[]{:S(2)}, u32[]{:S(2)}) collective-permute-start(f32[8,8,8,128]{3,2,1,0:T(8,128)S(1)} %total.1.refs_3_.refs_4_), channel_id=1, source_target_pairs={{0,16},{8,24},{16,0},{24,8},{1,17},{9,25},{17,1},{25,9},{2,18},{10... | collective-permute-start | bytes 786440 | tf_op jit(solution)/shard_map/ppermute | solution.py:416
  25.9 0.5 %collective-permute-start.2 = (f32[2,128,128]{2,1,0:T(8,128)S(1)}, f32[2,128,128]{2,1,0:T(8,128)S(1)}, u32[]{:S(2)}, u32[]{:S(2)}) collective-permute-start(f32[2,128,128]{2,1,0:T(8,128)S(1)} %collective-permute-done.1.refs_5_.refs_2_), channel_id=1, source_target_pairs={{0,8},{8,0},{16,24},{24,16},{1,9},{9,1},{17,25},{25,17},{2,10},{10... | collective-permute-start | bytes 393224 | tf_op jit(solution)/shard_map/ppermute | solution.py:416
  26.4 2.7 %march.6 = (f32[8,16,8,8,128]{4,3,2,1,0:T(8,128)S(1)}, f32[8,8,8,128]{3,2,1,0:T(8,128)S(1)}) custom-call(f32[56,8,128]{2,1,0:T(8,128)S(1)} %get-tuple-element.39.refs_0_, f32[16,256,128]{2,1,0:T(8,128)S(1)} %get-tuple-element.42.refs_1_, bf16[16,256,128]{2,1,0:T(8,128)(2,1)S(1)} %get-tuple-element.43.refs_2_, f32[8,8,8,128]{3,2,1,0:T(8,128)S(1)} %total.1.refs_3_.refs_4_, ...), custom_call_target="tpu_custom_call" | custom-call | flops 100000000 | bytes 1048576 | tf_op jit(solution)/shard_map/march/pallas_call | solution.py:64
  29.1 0.0 collective-permute-done.2.refs_6_.refs_3_
  29.1 2.7 %march.7 = (f32[8,16,8,8,128]{4,3,2,1,0:T(8,128)S(1)}, f32[8,8,8,128]{3,2,1,0:T(8,128)S(1)}) custom-call(f32[56,8,128]{2,1,0:T(8,128)S(1)} %get-tuple-element.39.refs_0_, f32[16,256,128]{2,1,0:T(8,128)S(1)} %get-tuple-element.42.refs_1_, bf16[16,256,128]{2,1,0:T(8,128)(2,1)S(1)} %get-tuple-element.43.refs_2_, f32[8,8,8,128]{3,2,1,0:T(8,128)S(1)} %total.1.refs_3_.refs_4_, ...), custom_call_target="tpu_custom_call" | custom-call | flops 100000000 | bytes 1048576 | tf_op jit(solution)/shard_map/march/pallas_call | solution.py:64
  31.8 0.4 dim.3
  32.2 0.1 collective-permute-start.11
  32.2 0.0 collective-permute-done.13.refs_1_
  32.3 0.5 %collective-permute-start.15 = (f32[8,8,8,128]{3,2,1,0:T(8,128)S(1)}, f32[8,8,8,128]{3,2,1,0:T(8,128)S(1)}, u32[]{:S(2)}, u32[]{:S(2)}) collective-permute-start(f32[8,8,8,128]{3,2,1,0:T(8,128)S(1)} %get-tuple-element.58.refs_1_.refs_5_), channel_id=1, source_target_pairs={{0,8},{8,0},{16,24},{24,16},{1,9},{9,1},{17,25},{25,17},{2,10},{10... | collective-permute-start | bytes 786440 | tf_op jit(solution)/shard_map/ppermute | solution.py:416
  32.8 0.1 collective-permute-start.16
  33.0 0.8 %collective-permute-done.11.refs_1_ = f32[8,8,8,128]{3,2,1,0:T(8,128)S(1)} collective-permute-done((f32[8,8,8,128]{3,2,1,0:T(8,128)S(1)}, f32[8,8,8,128]{3,2,1,0:T(8,128)S(1)}, u32[]{:S(2)}, u32[]{:S(2)}) %collective-permute-start.11) | collective-permute-done | bytes 262176 | tf_op jit(solution)/shard_map/ppermute | solution.py:416
  33.8 0.6 %collective-permute-start.14 = (f32[4,8,8,128]{3,2,1,0:T(8,128)S(1)}, f32[4,8,8,128]{3,2,1,0:T(8,128)S(1)}, u32[]{:S(2)}, u32[]{:S(2)}) collective-permute-start(f32[4,8,8,128]{3,2,1,0:T(8,128)S(1)} %get-tuple-element.60), channel_id=1, source_target_pairs={{0,1},{1,0},{2,3},{3,2},{4,5},{5,4},{6,7},{7,6},{8,9},{9,8},{10,11... | collective-permute-start | bytes 393224 | tf_op jit(solution)/shard_map/ppermute | solution.py:416
  34.4 0.0 collective-permute-done.15.refs_6_
  34.4 0.1 collective-permute-done.16.refs_8_
  34.5 0.4 pull.1.refs_2_.refs_9_
  34.9 0.3 collective-permute-start.20
  35.2 0.5 %collective-permute-start.21 = (f32[2,128,128]{2,1,0:T(8,128)S(1)}, f32[2,128,128]{2,1,0:T(8,128)S(1)}, u32[]{:S(2)}, u32[]{:S(2)}) collective-permute-start(f32[2,128,128]{2,1,0:T(8,128)S(1)} %pull.1.refs_2_.refs_9_), channel_id=1, source_target_pairs={{0,16},{8,24},{16,0},{24,8},{1,17},{9,25},{17,1},{25,9},{2,18},{10... | collective-permute-start | bytes 393224 | tf_op jit(solution)/shard_map/ppermute | solution.py:416
  35.7 1.1 %collective-permute-start.22 = (f32[2,128,128]{2,1,0:T(8,128)S(1)}, f32[2,128,128]{2,1,0:T(8,128)S(1)}, u32[]{:S(2)}, u32[]{:S(2)}) collective-permute-start(f32[2,128,128]{2,1,0:T(8,128)S(1)} %pull.1.refs_2_.refs_9_), channel_id=1, source_target_pairs={{0,24},{8,16},{16,8},{24,0},{1,25},{9,17},{17,9},{25,1},{2,26},{10... | collective-permute-start | bytes 393224 | tf_op jit(solution)/shard_map/ppermute | solution.py:416
  36.8 2.6 %collective-permute-done.14.refs_1_ = f32[4,8,8,128]{3,2,1,0:T(8,128)S(1)} collective-permute-done((f32[4,8,8,128]{3,2,1,0:T(8,128)S(1)}, f32[4,8,8,128]{3,2,1,0:T(8,128)S(1)}, u32[]{:S(2)}, u32[]{:S(2)}) %collective-permute-start.14) | collective-permute-done | bytes 131104 | tf_op jit(solution)/shard_map/ppermute | solution.py:416
  39.4 0.7 %collective-permute-start.17 = (f32[2,8,8,128]{3,2,1,0:T(8,128)S(1)}, f32[2,8,8,128]{3,2,1,0:T(8,128)S(1)}, u32[]{:S(2)}, u32[]{:S(2)}) collective-permute-start(f32[2,8,8,128]{3,2,1,0:T(8,128)S(1)} %get-tuple-element.63), channel_id=1, source_target_pairs={{0,2},{1,3},{2,0},{3,1},{4,6},{5,7},{6,4},{7,5},{8,10},{9,11},{10,... | collective-permute-start | bytes 196616 | tf_op jit(solution)/shard_map/ppermute | solution.py:416
  40.1 3.5 %collective-permute-start.18 = (f32[2,8,8,128]{3,2,1,0:T(8,128)S(1)}, f32[2,8,8,128]{3,2,1,0:T(8,128)S(1)}, u32[]{:S(2)}, u32[]{:S(2)}) collective-permute-start(f32[2,8,8,128]{3,2,1,0:T(8,128)S(1)} %get-tuple-element.64), channel_id=1, source_target_pairs={{0,4},{1,5},{2,6},{3,7},{4,0},{5,1},{6,2},{7,3},{8,12},{9,13},{10,... | collective-permute-start | bytes 196616 | tf_op jit(solution)/shard_map/ppermute | solution.py:416
  43.6 0.0 collective-permute-done.20.refs_10_
  43.6 0.3 collective-permute-start.19
  43.9 0.0 collective-permute-done.21.refs_11_
  43.9 2.4 %blend.1 = (f32[16,256,128]{2,1,0:T(8,128)}, f32[8,128]{1,0:T(8,128)S(1)}) custom-call(f32[56,8,128]{2,1,0:T(8,128)S(1)} %get-tuple-element.39.refs_0_, f32[8,8,8,128]{3,2,1,0:T(8,128)S(1)} %get-tuple-element.66.refs_1_, f32[8,8,8,128]{3,2,1,0:T(8,128)S(1)} %get-tuple-element.67.refs_2_, f32[8,8,8,128]{3,2,1,0:T(8,128)S(1)} %get-tuple-element.68.refs_3_, ...), custom_call_target="tpu_custom_call" | custom-call | flops 2400000000 | bytes 1048576 | tf_op jit(solution)/shard_map/blend/pallas_call | solution.py:64
  46.3 1.4 %collective-permute-done.18.refs_2_ = f32[2,8,8,128]{3,2,1,0:T(8,128)S(1)} collective-permute-done((f32[2,8,8,128]{3,2,1,0:T(8,128)S(1)}, f32[2,8,8,128]{3,2,1,0:T(8,128)S(1)}, u32[]{:S(2)}, u32[]{:S(2)}) %collective-permute-start.18) | collective-permute-done | bytes 65568 | tf_op jit(solution)/shard_map/ppermute | solution.py:416
  47.7 2.0 %collective-permute-done.19.refs_3_ = f32[2,8,8,128]{3,2,1,0:T(8,128)S(1)} collective-permute-done((f32[2,8,8,128]{3,2,1,0:T(8,128)S(1)}, f32[2,8,8,128]{3,2,1,0:T(8,128)S(1)}, u32[]{:S(2)}, u32[]{:S(2)}) %collective-permute-start.19) | collective-permute-done | bytes 65568 | tf_op jit(solution)/shard_map/ppermute | solution.py:416
  49.7 0.8 %picture.1 = f32[8,8,1024]{2,1,0:T(8,128)} custom-call(f32[2,8,8,128]{3,2,1,0:T(8,128)S(1)} %get-tuple-element.62.refs_0_, f32[2,8,8,128]{3,2,1,0:T(8,128)S(1)} %collective-permute-done.17.refs_1_, f32[2,8,8,128]{3,2,1,0:T(8,128)S(1)} %collective-permute-done.18.refs_2_, f32[2,8,8,128]{3,2,1,0:T(8,128)S(1)} %collective-permute-done.19.refs_3_, ...), custom_call_target="tpu_custom_call" | custom-call | bytes 1048576 | tf_op jit(solution)/shard_map/picture/pallas_call | solution.py:64
  (16 shorter events, 0.2 us)
Async XLA Ops:
  3.9 10.4 %collective-permute-start.6 = (f32[2,8,8,128]{3,2,1,0:T(8,128)S(1)}, f32[2,8,8,128]{3,2,1,0:T(8,128)S(1)}, u32[]{:S(2)}, u32[]{:S(2)}) collective-permute-start(f32[2,8,8,128]{3,2,1,0:T(8,128)S(1)} %get-tuple-element.46), channel_id=1, source_target_pairs={{0,2},{1,3},{2,0},{3,1},{4,6},{5,7},{6,4},{7,5},{8,10},{9,11},{10,... | collective-permute-start | bytes 196616 | tf_op jit(solution)/shard_map/ppermute | solution.py:416
  7.0 7.3 %collective-permute-start.7 = (f32[2,8,8,128]{3,2,1,0:T(8,128)S(1)}, f32[2,8,8,128]{3,2,1,0:T(8,128)S(1)}, u32[]{:S(2)}, u32[]{:S(2)}) collective-permute-start(f32[2,8,8,128]{3,2,1,0:T(8,128)S(1)} %get-tuple-element.47), channel_id=1, source_target_pairs={{0,4},{1,5},{2,6},{3,7},{4,0},{5,1},{6,2},{7,3},{8,12},{9,13},{10,... | collective-permute-start | bytes 196616 | tf_op jit(solution)/shard_map/ppermute | solution.py:416
  9.6 6.1 %collective-permute-start.8 = (f32[2,8,8,128]{3,2,1,0:T(8,128)S(1)}, f32[2,8,8,128]{3,2,1,0:T(8,128)S(1)}, u32[]{:S(2)}, u32[]{:S(2)}) collective-permute-start(f32[2,8,8,128]{3,2,1,0:T(8,128)S(1)} %get-tuple-element.48), channel_id=1, source_target_pairs={{0,6},{1,7},{2,4},{3,5},{4,2},{5,3},{6,0},{7,1},{8,14},{9,15},{10,... | collective-permute-start | bytes 196616 | tf_op jit(solution)/shard_map/ppermute | solution.py:416
  9.6 8.2 %collective-permute-start.1 = (f32[2,128,128]{2,1,0:T(8,128)S(1)}, f32[2,128,128]{2,1,0:T(8,128)S(1)}, u32[]{:S(2)}, u32[]{:S(2)}) collective-permute-start(f32[2,128,128]{2,1,0:T(8,128)S(1)} %get-tuple-element.41), channel_id=1, source_target_pairs={{0,16},{8,24},{16,0},{24,8},{1,17},{9,25},{17,1},{25,9},{2,18},{10... | collective-permute-start | bytes 393224 | tf_op jit(solution)/shard_map/ppermute | solution.py:416
  11.3 6.2 %collective-permute-start.4 = (f32[2,128,128]{2,1,0:T(8,128)S(1)}, f32[2,128,128]{2,1,0:T(8,128)S(1)}, u32[]{:S(2)}, u32[]{:S(2)}) collective-permute-start(f32[2,128,128]{2,1,0:T(8,128)S(1)} %get-tuple-element.40), channel_id=1, source_target_pairs={{0,16},{8,24},{16,0},{24,8},{1,17},{9,25},{17,1},{25,9},{2,18},{10... | collective-permute-start | bytes 393224 | tf_op jit(solution)/shard_map/ppermute | solution.py:416
  15.7 7.0 %collective-permute-start.10 = (f32[8,8,8,128]{3,2,1,0:T(8,128)S(1)}, f32[8,8,8,128]{3,2,1,0:T(8,128)S(1)}, u32[]{:S(2)}, u32[]{:S(2)}) collective-permute-start(f32[8,8,8,128]{3,2,1,0:T(8,128)S(1)} %turn.6.refs_3_.refs_0_), channel_id=1, source_target_pairs={{0,16},{8,24},{16,0},{24,8},{1,17},{9,25},{17,1},{25,9},{2,18},{10... | collective-permute-start | bytes 786440 | tf_op jit(solution)/shard_map/ppermute | solution.py:416
  17.2 3.2 %collective-permute-start.3 = (f32[2,128,128]{2,1,0:T(8,128)S(1)}, f32[2,128,128]{2,1,0:T(8,128)S(1)}, u32[]{:S(2)}, u32[]{:S(2)}) collective-permute-start(f32[2,128,128]{2,1,0:T(8,128)S(1)} %get-tuple-element.41), channel_id=1, source_target_pairs={{0,8},{8,0},{16,24},{24,16},{1,9},{9,1},{17,25},{25,17},{2,10},{10... | collective-permute-start | bytes 393224 | tf_op jit(solution)/shard_map/ppermute | solution.py:416
  17.5 2.9 %collective-permute-start.5 = (f32[2,128,128]{2,1,0:T(8,128)S(1)}, f32[2,128,128]{2,1,0:T(8,128)S(1)}, u32[]{:S(2)}, u32[]{:S(2)}) collective-permute-start(f32[2,128,128]{2,1,0:T(8,128)S(1)} %collective-permute-done.4.refs_2_), channel_id=1, source_target_pairs={{0,8},{8,0},{16,24},{24,16},{1,9},{9,1},{17,25},{25,17},{2,10},{10... | collective-permute-start | bytes 393224 | tf_op jit(solution)/shard_map/ppermute | solution.py:416
  20.8 3.5 %collective-permute-start.9 = (f32[8,8,8,128]{3,2,1,0:T(8,128)S(1)}, f32[8,8,8,128]{3,2,1,0:T(8,128)S(1)}, u32[]{:S(2)}, u32[]{:S(2)}) collective-permute-start(f32[8,8,8,128]{3,2,1,0:T(8,128)S(1)} %get-tuple-element.51.refs_4_), channel_id=1, source_target_pairs={{0,8},{8,0},{16,24},{24,16},{1,9},{9,1},{17,25},{25,17},{2,10},{10... | collective-permute-start | bytes 786440 | tf_op jit(solution)/shard_map/ppermute | solution.py:416
  22.7 9.5 %collective-permute-start.13 = (f32[8,8,8,128]{3,2,1,0:T(8,128)S(1)}, f32[8,8,8,128]{3,2,1,0:T(8,128)S(1)}, u32[]{:S(2)}, u32[]{:S(2)}) collective-permute-start(f32[8,8,8,128]{3,2,1,0:T(8,128)S(1)} %get-tuple-element.57), channel_id=1, source_target_pairs={{0,1},{1,0},{2,3},{3,2},{4,5},{5,4},{6,7},{7,6},{8,9},{9,8},{10,11... | collective-permute-start | bytes 786440 | tf_op jit(solution)/shard_map/ppermute | solution.py:416
  24.3 8.6 %collective-permute-start.12 = (f32[8,8,8,128]{3,2,1,0:T(8,128)S(1)}, f32[8,8,8,128]{3,2,1,0:T(8,128)S(1)}, u32[]{:S(2)}, u32[]{:S(2)}) collective-permute-start(f32[8,8,8,128]{3,2,1,0:T(8,128)S(1)} %total.1.refs_3_.refs_4_), channel_id=1, source_target_pairs={{0,16},{8,24},{16,0},{24,8},{1,17},{9,25},{17,1},{25,9},{2,18},{10... | collective-permute-start | bytes 786440 | tf_op jit(solution)/shard_map/ppermute | solution.py:416
  25.9 3.2 %collective-permute-start = (f32[2,128,128]{2,1,0:T(8,128)S(1)}, f32[2,128,128]{2,1,0:T(8,128)S(1)}, u32[]{:S(2)}, u32[]{:S(2)}) collective-permute-start(f32[2,128,128]{2,1,0:T(8,128)S(1)} %get-tuple-element.40), channel_id=1, source_target_pairs={{0,8},{8,0},{16,24},{24,16},{1,9},{9,1},{17,25},{25,17},{2,10},{10... | collective-permute-start | bytes 393224 | tf_op jit(solution)/shard_map/ppermute | solution.py:416
  25.9 3.2 %collective-permute-start.2 = (f32[2,128,128]{2,1,0:T(8,128)S(1)}, f32[2,128,128]{2,1,0:T(8,128)S(1)}, u32[]{:S(2)}, u32[]{:S(2)}) collective-permute-start(f32[2,128,128]{2,1,0:T(8,128)S(1)} %collective-permute-done.1.refs_5_.refs_2_), channel_id=1, source_target_pairs={{0,8},{8,0},{16,24},{24,16},{1,9},{9,1},{17,25},{25,17},{2,10},{10... | collective-permute-start | bytes 393224 | tf_op jit(solution)/shard_map/ppermute | solution.py:416
  32.2 1.6 %collective-permute-start.11 = (f32[8,8,8,128]{3,2,1,0:T(8,128)S(1)}, f32[8,8,8,128]{3,2,1,0:T(8,128)S(1)}, u32[]{:S(2)}, u32[]{:S(2)}) collective-permute-start(f32[8,8,8,128]{3,2,1,0:T(8,128)S(1)} %get-tuple-element.56.refs_2_), channel_id=1, source_target_pairs={{0,8},{8,0},{16,24},{24,16},{1,9},{9,1},{17,25},{25,17},{2,10},{10... | collective-permute-start | bytes 786440 | tf_op jit(solution)/shard_map/ppermute | solution.py:416
  32.3 2.1 %collective-permute-start.15 = (f32[8,8,8,128]{3,2,1,0:T(8,128)S(1)}, f32[8,8,8,128]{3,2,1,0:T(8,128)S(1)}, u32[]{:S(2)}, u32[]{:S(2)}) collective-permute-start(f32[8,8,8,128]{3,2,1,0:T(8,128)S(1)} %get-tuple-element.58.refs_1_.refs_5_), channel_id=1, source_target_pairs={{0,8},{8,0},{16,24},{24,16},{1,9},{9,1},{17,25},{25,17},{2,10},{10... | collective-permute-start | bytes 786440 | tf_op jit(solution)/shard_map/ppermute | solution.py:416
  32.8 1.7 %collective-permute-start.16 = (f32[8,8,8,128]{3,2,1,0:T(8,128)S(1)}, f32[8,8,8,128]{3,2,1,0:T(8,128)S(1)}, u32[]{:S(2)}, u32[]{:S(2)}) collective-permute-start(f32[8,8,8,128]{3,2,1,0:T(8,128)S(1)} %get-tuple-element.61.refs_7_), channel_id=1, source_target_pairs={{0,8},{8,0},{16,24},{24,16},{1,9},{9,1},{17,25},{25,17},{2,10},{10... | collective-permute-start | bytes 786440 | tf_op jit(solution)/shard_map/ppermute | solution.py:416
  33.8 5.6 %collective-permute-start.14 = (f32[4,8,8,128]{3,2,1,0:T(8,128)S(1)}, f32[4,8,8,128]{3,2,1,0:T(8,128)S(1)}, u32[]{:S(2)}, u32[]{:S(2)}) collective-permute-start(f32[4,8,8,128]{3,2,1,0:T(8,128)S(1)} %get-tuple-element.60), channel_id=1, source_target_pairs={{0,1},{1,0},{2,3},{3,2},{4,5},{5,4},{6,7},{7,6},{8,9},{9,8},{10,11... | collective-permute-start | bytes 393224 | tf_op jit(solution)/shard_map/ppermute | solution.py:416
  34.9 8.7 %collective-permute-start.20 = (f32[2,128,128]{2,1,0:T(8,128)S(1)}, f32[2,128,128]{2,1,0:T(8,128)S(1)}, u32[]{:S(2)}, u32[]{:S(2)}) collective-permute-start(f32[2,128,128]{2,1,0:T(8,128)S(1)} %pull.1.refs_2_.refs_9_), channel_id=1, source_target_pairs={{0,8},{8,0},{16,24},{24,16},{1,9},{9,1},{17,25},{25,17},{2,10},{10... | collective-permute-start | bytes 393224 | tf_op jit(solution)/shard_map/ppermute | solution.py:416
  35.2 8.7 %collective-permute-start.21 = (f32[2,128,128]{2,1,0:T(8,128)S(1)}, f32[2,128,128]{2,1,0:T(8,128)S(1)}, u32[]{:S(2)}, u32[]{:S(2)}) collective-permute-start(f32[2,128,128]{2,1,0:T(8,128)S(1)} %pull.1.refs_2_.refs_9_), channel_id=1, source_target_pairs={{0,16},{8,24},{16,0},{24,8},{1,17},{9,25},{17,1},{25,9},{2,18},{10... | collective-permute-start | bytes 393224 | tf_op jit(solution)/shard_map/ppermute | solution.py:416
  35.7 8.1 %collective-permute-start.22 = (f32[2,128,128]{2,1,0:T(8,128)S(1)}, f32[2,128,128]{2,1,0:T(8,128)S(1)}, u32[]{:S(2)}, u32[]{:S(2)}) collective-permute-start(f32[2,128,128]{2,1,0:T(8,128)S(1)} %pull.1.refs_2_.refs_9_), channel_id=1, source_target_pairs={{0,24},{8,16},{16,8},{24,0},{1,25},{9,17},{17,9},{25,1},{2,26},{10... | collective-permute-start | bytes 393224 | tf_op jit(solution)/shard_map/ppermute | solution.py:416
  39.4 6.9 %collective-permute-start.17 = (f32[2,8,8,128]{3,2,1,0:T(8,128)S(1)}, f32[2,8,8,128]{3,2,1,0:T(8,128)S(1)}, u32[]{:S(2)}, u32[]{:S(2)}) collective-permute-start(f32[2,8,8,128]{3,2,1,0:T(8,128)S(1)} %get-tuple-element.63), channel_id=1, source_target_pairs={{0,2},{1,3},{2,0},{3,1},{4,6},{5,7},{6,4},{7,5},{8,10},{9,11},{10,... | collective-permute-start | bytes 196616 | tf_op jit(solution)/shard_map/ppermute | solution.py:416
  40.1 7.6 %collective-permute-start.18 = (f32[2,8,8,128]{3,2,1,0:T(8,128)S(1)}, f32[2,8,8,128]{3,2,1,0:T(8,128)S(1)}, u32[]{:S(2)}, u32[]{:S(2)}) collective-permute-start(f32[2,8,8,128]{3,2,1,0:T(8,128)S(1)} %get-tuple-element.64), channel_id=1, source_target_pairs={{0,4},{1,5},{2,6},{3,7},{4,0},{5,1},{6,2},{7,3},{8,12},{9,13},{10,... | collective-permute-start | bytes 196616 | tf_op jit(solution)/shard_map/ppermute | solution.py:416
  43.6 6.1 %collective-permute-start.19 = (f32[2,8,8,128]{3,2,1,0:T(8,128)S(1)}, f32[2,8,8,128]{3,2,1,0:T(8,128)S(1)}, u32[]{:S(2)}, u32[]{:S(2)}) collective-permute-start(f32[2,8,8,128]{3,2,1,0:T(8,128)S(1)} %get-tuple-element.65), channel_id=1, source_target_pairs={{0,6},{1,7},{2,4},{3,5},{4,2},{5,3},{6,0},{7,1},{8,14},{9,15},{10,... | collective-permute-start | bytes 196616 | tf_op jit(solution)/shard_map/ppermute | solution.py:416

commit v2 on v1

--- a/solution.py
+++ b/solution.py
@@ -157,7 +157,7 @@
 def march(consts, thermal, soot_share, bands, share, o, ties, us):
     cells, _, columns = thermal.shape
 
-    def kernel(const_ref, thermal_ref, soot_ref, part_ref, light_ref):
+    def kernel(const_ref, thermal_ref, soot_ref, fade_ref, source_ref, light_ref):
         first = (lax.axis_index("depth") ^ o) * share
 
         def tile(i, _):
@@ -173,23 +173,20 @@
                 heat = thermal_ref[k, here]
                 soot = soot_ref[k, here].astype(F32)
                 cold = pltpu.reciprocal(heat, approx=True)
-                cold2 = cold * cold
                 for b in range(bands):
                     fade = jnp.exp2(soot * const(SOOT_STEP, b) + heat * const(GAS_STEP, b))
                     source = pltpu.reciprocal(jnp.exp2(cold * const(PLANCK_STEP, b)) - 1.0, approx=True)
+                    fade_ref[2 * i, k, b] = fade[:ROWS]
+                    fade_ref[2 * i + 1, k, b] = fade[ROWS:]
+                    source_ref[2 * i, k, b] = source[:ROWS]
+                    source_ref[2 * i + 1, k, b] = source[ROWS:]
                     if k == 0:
-                        beyond = fade
-                        emitted = (1.0 - fade) * source
-                        local = source
+                        light[b] = (1.0 - fade) * source
+                        clear[b] = fade
                     else:
                         beyond = clear[b] * fade
-                        emitted = (clear[b] - beyond) * source
-                        local = clear[b] * source + light[b]
-                    part = (emitted + emitted * source) * (cold2 * const(RATIO, b)) + local
-                    part_ref[2 * i, k, b] = part[:ROWS]
-                    part_ref[2 * i + 1, k, b] = part[ROWS:]
-                    light[b] = emitted if k == 0 else light[b] + emitted
-                    clear[b] = beyond
+                        light[b] = light[b] + (clear[b] - beyond) * source
+                        clear[b] = beyond
             for b in range(bands):
                 light_ref[2 * i, b] = light[b][:ROWS]
                 light_ref[2 * i + 1, b] = light[b][ROWS:]
@@ -201,8 +198,8 @@
         kernel,
         "march",
         [vmem()] * 3,
-        [vmem()] * 2,
-        [shape(share, cells, bands, ROWS, columns), shape(share, bands, ROWS, columns)],
+        [vmem()] * 3,
+        [shape(share, cells, bands, ROWS, columns)] * 2 + [shape(share, bands, ROWS, columns)],
         us=us,
     )(consts, thermal, soot_share, ties=ties)
 
@@ -323,16 +320,68 @@
     )(consts, *seen, *tangents, ties=ties)
 
 
-def blend(consts, scales, tangents, pulls, parts, twisted, ties=()):
-    slabs = len(parts)
-    share, cells, bands, _, columns = parts[0].shape
+def bend_tile(const_ref, thermal_ref, fade_ref, source_ref, scale_ref, tangent_ref, g, here, twist, store):
+    _, cells, bands, _, _ = fade_ref.shape
+    clear = [tangent_ref[g ^ twist, b] * scale_ref[g, b] * const_ref[GAS * bands + b] for b in range(bands)]
+    passed = None
+    for k in range(cells):
+        steep = local = emitted = None
+        for b in range(bands):
+            glow = source_ref[g, k, b]
+            beyond = clear[b] * fade_ref[g, k, b]
+            given = (clear[b] - beyond) * glow
+            slope = (given + given * glow) * const_ref[RATIO * bands + b]
+            before = clear[b] * glow
+            steep = slope if steep is None else steep + slope
+            local = before if local is None else local + before
+            emitted = given if emitted is None else emitted + given
+            clear[b] = beyond
+        cold = pltpu.reciprocal(thermal_ref[k, here], approx=True)
+        total = steep * (cold * cold) + local
+        store(k, total if passed is None else total + passed)
+        passed = emitted if passed is None else passed + emitted
+
+
+def bend(consts, thermal, fade, source, scale, tangent, o, twisted, ties):
+    share, cells, _, _, columns = fade.shape
+
+    def kernel(const_ref, thermal_ref, fade_ref, source_ref, scale_ref, tangent_ref, out_ref):
+        first = (lax.axis_index("depth") ^ o) * share
+        twist = lax.axis_index("width") if twisted else 0
+
+        def tile(g, _):
+            def store(k, value):
+                out_ref[k, rows_at(g)] = value
+
+            bend_tile(
+                const_ref, thermal_ref, fade_ref, source_ref, scale_ref, tangent_ref,
+                g, rows_at(first + g), twist, store,
+            )
+            return 0
+
+        lax.fori_loop(0, share, tile, 0)
+
+    return kernel_call(
+        kernel, "bend", [vmem()] * 6, vmem(), shape(cells, share * ROWS, columns)
+    )(consts, thermal, fade, source, scale, tangent, ties=ties)
+
+
+def blend(consts, thermal, scales, tangents, pulls, fades, sources, bent, twisted, ties=()):
+    slabs = len(pulls)
+    cells, _, columns = thermal.shape
+    share, bands, _, _ = scales[0].shape
     half = slabs // 2
-
-    def kernel(const_ref, *refs):
-        scale_refs, tangent_refs, pull_refs, part_refs = (
-            refs[i * slabs : (i + 1) * slabs] for i in range(4)
-        )
-        out_hbm, token_ref, gradient_ref, sems = refs[4 * slabs :]
+    made = [o for o in range(slabs) if o not in bent]
+
+    def kernel(const_ref, thermal_ref, *refs):
+        refs = list(refs)
+
+        def take(names):
+            return {o: refs.pop(0) for o in names}
+
+        pull_refs, bent_refs = take(range(slabs)), take(bent)
+        scale_refs, tangent_refs, fade_refs, source_refs = (take(made) for _ in range(4))
+        out_hbm, token_ref, gradient_ref, sems = refs
         token_ref[...] = jnp.zeros_like(token_ref)
         mine = lax.axis_index("depth")
         twist = lax.axis_index("width") if twisted else 0
@@ -341,20 +390,23 @@
 
             def tile(g, _, o=o):
                 here = rows_at(((mine ^ o) & (half - 1)) * share + g)
-                weight = [
-                    tangent_refs[o][g ^ twist, b] * scale_refs[o][g, b] * const_ref[GAS * bands + b]
-                    for b in range(bands)
-                ]
                 away = None
                 for j in range(slabs):
                     side = (o // half) ^ (j // half)
                     term = pull_refs[j][side, here] * const_ref[KINDS * bands + slabs + j]
                     away = term if away is None else away + term
-                for k in range(cells):
-                    total = part_refs[o][g, k, 0] * weight[0] - away
-                    for b in range(1, bands):
-                        total = total + part_refs[o][g, k, b] * weight[b]
-                    gradient_ref[o, k, rows_at(g)] = total
+
+                def store(k, value):
+                    gradient_ref[o, k, rows_at(g)] = value - away
+
+                if o in bent_refs:
+                    for k in range(cells):
+                        store(k, bent_refs[o][k, rows_at(g)])
+                else:
+                    bend_tile(
+                        const_ref, thermal_ref, fade_refs[o], source_refs[o], scale_refs[o], tangent_refs[o],
+                        g, rows_at((mine ^ o) * share + g), twist, store,
+                    )
                 return 0
 
             lax.fori_loop(0, share, tile, 0)
@@ -365,16 +417,19 @@
             copy.wait()
 
     height = share * ROWS
+    operands = [consts, thermal, *pulls, *bent.values()]
+    for some in (scales, tangents, fades, sources):
+        operands += [some[o] for o in made]
     return kernel_call(
         kernel,
         "blend",
-        [vmem()] * (1 + 4 * slabs),
+        [vmem()] * len(operands),
         [hbm(), vmem()],
         [shape(cells, slabs * height, columns), shape(ROWS, columns)],
         us=BLEND_US,
         mebibytes=8,
         scratch=[pltpu.VMEM((slabs, cells, height, columns), F32), pltpu.SemaphoreType.DMA((slabs,))],
-    )(consts, *scales, *tangents, *pulls, *parts, ties=ties)
+    )(*operands, ties=ties)
 
 
 def picture(sources, ties=()):
@@ -454,10 +509,10 @@
             blocks = twist(lined.transpose(1, 0, 2, 3))
             return blocks[0::2], blocks[1::2]
 
-        parts, lights, scales, seen = {}, {}, {}, {}
+        fades, sources, lights, scales, seen = {}, {}, {}, {}, {}
 
         def lit(o, us, *ties):
-            parts[o], lights[o] = march(consts, heat, soot, bands, share, o, ties, us)
+            fades[o], sources[o], lights[o] = march(consts, heat, soot, bands, share, o, ties, us)
             return lights[o]
 
         def dimmed(shares, paths, *ties):
@@ -504,11 +559,11 @@
         odd = swap(odd, 1, "width")
         near_paths = spread(near_sums) | spread(across_near, True)
         cores = [near_paths[o] for o in near_paths if o not in (0, top)]
-        seen_far = total(lower([seen[o] for o in far]), (even,))
+        seen_far = total(lower([seen[o] for o in far]), (even, *cores))
         across = swap(seen_far, top)
         done = seen_far
         for o in near:
-            done = lit(o, NEAR_US, seen_far, done, *(cores if o else ()))
+            done = lit(o, NEAR_US, seen_far, done)
         dimmed(near, near_paths, done)
         seen_near = lower([seen[o] for o in near])
         blocks = turn(
@@ -523,12 +578,14 @@
             consts, [seen[o] for o in range(slabs)], [tangents[o] for o in range(slabs)], whole, (image[0],)
         )
         pulls = {o: swap(pulled, o) if o else pulled for o in range(slabs)}
-        image = turn([(image[0], evens), (odd, odds)], groups, (pulled,))
+        bent = {
+            o: bend(consts, heat, fades[o], sources[o], scales[o], tangents[o], o, whole, (pulled,))
+            for o in near[:1]
+        }
+        image = turn([(image[0], evens), (odd, odds)], groups, tuple(bent.values()))
         image = swap_groups(image)
         gradient, done = blend(
-            consts,
-            *([some[o] for o in range(slabs)] for some in (scales, tangents, pulls, parts)),
-            whole,
+            consts, heat, scales, tangents, [pulls[o] for o in range(slabs)], fades, sources, bent, whole
         )
         return picture(list(zip(image, groups)), (done,)), gradient
 

time: 50.6 us -> 48.8 us (0.964)
  waiting for transfers between devices: 10.1 us -> 6.22 us
  Pallas kernels: 18.4 us -> 20.3 us
    ppermute x23, waiting for transfers between devices: 10.1 us -> 6.22 us  [swap(): return lax.ppermute(value, axis, pairs)]
    pallas_call x18 -> x19, Pallas kernels: 18.4 us -> 20.3 us  [run(): call(*[pltpu.with_memory_space_constraint(x, pltpu.VMEM) if held(spec) el...]
  transfers between devices with their start and end apart: 23 -> 23, of which waited for: 8 -> 7; matrix products, arithmetic and copies ran while one was open for 0% -> 0% of each run, Pallas kernels for 29% -> 34%
where the time goes in v2:
time: 48.8 us; the launch traced here: 48.6 us
  starting transfers between devices  21.2 us (43%)
  Pallas kernels  20.3 us (42%)
  waiting for transfers between devices  6.22 us (13%)
  between operations  0.8 us (2%)
    ppermute x23, starting transfers between devices, swap(): return lax.ppermute(value, axis, pairs)  21.2 us
    pallas_call x19, Pallas kernels, run(): call(*[pltpu.with_memory_space_constraint(x, pltpu.VMEM) if held(spec) el...  20.3 us
    ppermute x23, waiting for transfers between devices, swap(): return lax.ppermute(value, axis, pairs)  6.22 us
  transfers between devices with their start and end apart: 23, of which 7 were waited for; matrix products, arithmetic and copies ran while one was open for 0% of the time, Pallas kernels for 34%

profile of v2, /device:TPU:0, one launch (start us, length us, event | category | flops | bytes accessed | tf_op | source)
XLA Modules:
  0.0 48.6 jit_solution(1533654906687792902)
XLA Ops:
  0.6 3.2 %load.1 = (f32[16,256,128]{2,1,0:T(8,128)S(1)}, bf16[16,256,128]{2,1,0:T(8,128)(2,1)S(1)}, f32[2,128,128]{2,1,0:T(8,128)S(1)}, f32[2,128,128]{2,1,0:T(8,128)S(1)...) custom-call(f32[8]{0:T(128)} %refs_0_.1, ...), custom_call_target="tpu_custom_call" | custom-call | bytes 1048576 | tf_op jit(solution)/shard_map/load/pallas_call | solution.py:64
  3.9 3.1 %collective-permute-start.6 = (f32[2,8,8,128]{3,2,1,0:T(8,128)S(1)}, f32[2,8,8,128]{3,2,1,0:T(8,128)S(1)}, u32[]{:S(2)}, u32[]{:S(2)}) collective-permute-start(f32[2,8,8,128]{3,2,1,0:T(8,128)S(1)} %get-tuple-element.50), channel_id=1, source_target_pairs={{0,2},{1,3},{2,0},{3,1},{4,6},{5,7},{6,4},{7,5},{8,10},{9,11},{10,... | collective-permute-start | bytes 196616 | tf_op jit(solution)/shard_map/ppermute | solution.py:471
  7.0 2.6 %collective-permute-start.7 = (f32[2,8,8,128]{3,2,1,0:T(8,128)S(1)}, f32[2,8,8,128]{3,2,1,0:T(8,128)S(1)}, u32[]{:S(2)}, u32[]{:S(2)}) collective-permute-start(f32[2,8,8,128]{3,2,1,0:T(8,128)S(1)} %get-tuple-element.51), channel_id=1, source_target_pairs={{0,4},{1,5},{2,6},{3,7},{4,0},{5,1},{6,2},{7,3},{8,12},{9,13},{10,... | collective-permute-start | bytes 196616 | tf_op jit(solution)/shard_map/ppermute | solution.py:471
  9.6 1.7 %collective-permute-start.1 = (f32[2,128,128]{2,1,0:T(8,128)S(1)}, f32[2,128,128]{2,1,0:T(8,128)S(1)}, u32[]{:S(2)}, u32[]{:S(2)}) collective-permute-start(f32[2,128,128]{2,1,0:T(8,128)S(1)} %get-tuple-element.45), channel_id=1, source_target_pairs={{0,16},{8,24},{16,0},{24,8},{1,17},{9,25},{17,1},{25,9},{2,18},{10... | collective-permute-start | bytes 393224 | tf_op jit(solution)/shard_map/ppermute | solution.py:471
  11.3 0.3 collective-permute-start.4
  11.6 2.0 %march.4 = (f32[8,16,8,8,128]{4,3,2,1,0:T(8,128)S(1)}, f32[8,16,8,8,128]{4,3,2,1,0:T(8,128)S(1)}, f32[8,8,8,128]{3,2,1,0:T(8,128)S(1)}) custom-call(f32[56,8,128]{2,1,0:T(8,128)S(1)} %get-tuple-element.43.refs_0_, f32[16,256,128]{2,1,0:T(8,128)S(1)} %get-tuple-element.46.refs_1_, bf16[16,256,128]{2,1,0:T(8,128)(2,1)S(1)} %get-tuple-element.47.refs_2_), custom_call_target="tpu_custom_call" | custom-call | flops 2400000000 | bytes 1048576 | tf_op jit(solution)/shard_map/march/pallas_call | solution.py:64
  13.6 0.0 collective-permute-done.6.refs_1_
  13.6 0.6 %collective-permute-done.7.refs_2_ = f32[2,8,8,128]{3,2,1,0:T(8,128)S(1)} collective-permute-done((f32[2,8,8,128]{3,2,1,0:T(8,128)S(1)}, f32[2,8,8,128]{3,2,1,0:T(8,128)S(1)}, u32[]{:S(2)}, u32[]{:S(2)}) %collective-permute-start.7) | collective-permute-done | bytes 65568 | tf_op jit(solution)/shard_map/ppermute | solution.py:471
  14.2 1.4 %collective-permute-done.8.refs_3_ = f32[2,8,8,128]{3,2,1,0:T(8,128)S(1)} collective-permute-done((f32[2,8,8,128]{3,2,1,0:T(8,128)S(1)}, f32[2,8,8,128]{3,2,1,0:T(8,128)S(1)}, u32[]{:S(2)}, u32[]{:S(2)}) %collective-permute-start.8) | collective-permute-done | bytes 65568 | tf_op jit(solution)/shard_map/ppermute | solution.py:471
  15.7 1.6 %collective-permute-start.10 = (f32[8,8,8,128]{3,2,1,0:T(8,128)S(1)}, f32[8,8,8,128]{3,2,1,0:T(8,128)S(1)}, u32[]{:S(2)}, u32[]{:S(2)}) collective-permute-start(f32[8,8,8,128]{3,2,1,0:T(8,128)S(1)} %turn.6.refs_3_.refs_0_), channel_id=1, source_target_pairs={{0,16},{8,24},{16,0},{24,8},{1,17},{9,25},{17,1},{25,9},{2,18},{10... | collective-permute-start | bytes 786440 | tf_op jit(solution)/shard_map/ppermute | solution.py:471
  17.2 0.0 collective-permute-start.3
  17.2 0.5 %collective-permute-start = (f32[2,128,128]{2,1,0:T(8,128)S(1)}, f32[2,128,128]{2,1,0:T(8,128)S(1)}, u32[]{:S(2)}, u32[]{:S(2)}) collective-permute-start(f32[2,128,128]{2,1,0:T(8,128)S(1)} %get-tuple-element.44), channel_id=1, source_target_pairs={{0,8},{8,0},{16,24},{24,16},{1,9},{9,1},{17,25},{25,17},{2,10},{10... | collective-permute-start | bytes 393224 | tf_op jit(solution)/shard_map/ppermute | solution.py:471
  17.7 0.0 collective-permute-start.5
  17.7 0.0 collective-permute-done.1.refs_5_.refs_2_
  17.7 0.5 %collective-permute-start.2 = (f32[2,128,128]{2,1,0:T(8,128)S(1)}, f32[2,128,128]{2,1,0:T(8,128)S(1)}, u32[]{:S(2)}, u32[]{:S(2)}) collective-permute-start(f32[2,128,128]{2,1,0:T(8,128)S(1)} %collective-permute-done.1.refs_5_.refs_2_), channel_id=1, source_target_pairs={{0,8},{8,0},{16,24},{24,16},{1,9},{9,1},{17,25},{25,17},{2,10},{10... | collective-permute-start | bytes 393224 | tf_op jit(solution)/shard_map/ppermute | solution.py:471
  18.2 2.0 %march.5 = (f32[8,16,8,8,128]{4,3,2,1,0:T(8,128)S(1)}, f32[8,16,8,8,128]{4,3,2,1,0:T(8,128)S(1)}, f32[8,8,8,128]{3,2,1,0:T(8,128)S(1)}) custom-call(f32[56,8,128]{2,1,0:T(8,128)S(1)} %get-tuple-element.43.refs_0_, f32[16,256,128]{2,1,0:T(8,128)S(1)} %get-tuple-element.46.refs_1_, bf16[16,256,128]{2,1,0:T(8,128)(2,1)S(1)} %get-tuple-element.47.refs_2_, ...), custom_call_target="tpu_custom_call" | custom-call | flops 2400000000 | bytes 1048576 | tf_op jit(solution)/shard_map/march/pallas_call | solution.py:64
  20.2 0.4 dim.2
  20.6 0.1 collective-permute-start.9
  20.8 1.9 %collective-permute-done.10.refs_1_ = f32[8,8,8,128]{3,2,1,0:T(8,128)S(1)} collective-permute-done((f32[8,8,8,128]{3,2,1,0:T(8,128)S(1)}, f32[8,8,8,128]{3,2,1,0:T(8,128)S(1)}, u32[]{:S(2)}, u32[]{:S(2)}) %collective-permute-start.10) | collective-permute-done | bytes 262176 | tf_op jit(solution)/shard_map/ppermute | solution.py:471
  22.7 1.6 %collective-permute-start.13 = (f32[8,8,8,128]{3,2,1,0:T(8,128)S(1)}, f32[8,8,8,128]{3,2,1,0:T(8,128)S(1)}, u32[]{:S(2)}, u32[]{:S(2)}) collective-permute-start(f32[8,8,8,128]{3,2,1,0:T(8,128)S(1)} %get-tuple-element.61), channel_id=1, source_target_pairs={{0,1},{1,0},{2,3},{3,2},{4,5},{5,4},{6,7},{7,6},{8,9},{9,8},{10,11... | collective-permute-start | bytes 786440 | tf_op jit(solution)/shard_map/ppermute | solution.py:471
  24.3 0.0 collective-permute-done.refs_3_.refs_1_
  24.3 0.0 collective-permute-done.2.refs_4_.refs_3_
  24.3 0.0 collective-permute-done.9.refs_1_
  24.3 1.6 %collective-permute-start.12 = (f32[8,8,8,128]{3,2,1,0:T(8,128)S(1)}, f32[8,8,8,128]{3,2,1,0:T(8,128)S(1)}, u32[]{:S(2)}, u32[]{:S(2)}) collective-permute-start(f32[8,8,8,128]{3,2,1,0:T(8,128)S(1)} %total.1.refs_3_.refs_4_), channel_id=1, source_target_pairs={{0,16},{8,24},{16,0},{24,8},{1,17},{9,25},{17,1},{25,9},{2,18},{10... | collective-permute-start | bytes 786440 | tf_op jit(solution)/shard_map/ppermute | solution.py:471
  25.9 1.9 %march.6 = (f32[8,16,8,8,128]{4,3,2,1,0:T(8,128)S(1)}, f32[8,16,8,8,128]{4,3,2,1,0:T(8,128)S(1)}, f32[8,8,8,128]{3,2,1,0:T(8,128)S(1)}) custom-call(f32[56,8,128]{2,1,0:T(8,128)S(1)} %get-tuple-element.43.refs_0_, f32[16,256,128]{2,1,0:T(8,128)S(1)} %get-tuple-element.46.refs_1_, bf16[16,256,128]{2,1,0:T(8,128)(2,1)S(1)} %get-tuple-element.47.refs_2_, ...), custom_call_target="tpu_custom_call" | custom-call | flops 100000000 | bytes 1048576 | tf_op jit(solution)/shard_map/march/pallas_call | solution.py:64
  27.8 1.9 %march.7 = (f32[8,16,8,8,128]{4,3,2,1,0:T(8,128)S(1)}, f32[8,16,8,8,128]{4,3,2,1,0:T(8,128)S(1)}, f32[8,8,8,128]{3,2,1,0:T(8,128)S(1)}) custom-call(f32[56,8,128]{2,1,0:T(8,128)S(1)} %get-tuple-element.43.refs_0_, f32[16,256,128]{2,1,0:T(8,128)S(1)} %get-tuple-element.46.refs_1_, bf16[16,256,128]{2,1,0:T(8,128)(2,1)S(1)} %get-tuple-element.47.refs_2_, ...), custom_call_target="tpu_custom_call" | custom-call | flops 100000000 | bytes 1048576 | tf_op jit(solution)/shard_map/march/pallas_call | solution.py:64
  29.8 0.4 dim.3
  30.2 0.1 collective-permute-start.11
  30.2 0.0 collective-permute-done.13.refs_1_
  30.3 0.5 %collective-permute-start.15 = (f32[8,8,8,128]{3,2,1,0:T(8,128)S(1)}, f32[8,8,8,128]{3,2,1,0:T(8,128)S(1)}, u32[]{:S(2)}, u32[]{:S(2)}) collective-permute-start(f32[8,8,8,128]{3,2,1,0:T(8,128)S(1)} %get-tuple-element.62.refs_1_.refs_5_), channel_id=1, source_target_pairs={{0,8},{8,0},{16,24},{24,16},{1,9},{9,1},{17,25},{25,17},{2,10},{10... | collective-permute-start | bytes 786440 | tf_op jit(solution)/shard_map/ppermute | solution.py:471
  30.8 0.1 collective-permute-start.16
  31.0 0.8 %collective-permute-done.11.refs_1_ = f32[8,8,8,128]{3,2,1,0:T(8,128)S(1)} collective-permute-done((f32[8,8,8,128]{3,2,1,0:T(8,128)S(1)}, f32[8,8,8,128]{3,2,1,0:T(8,128)S(1)}, u32[]{:S(2)}, u32[]{:S(2)}) %collective-permute-start.11) | collective-permute-done | bytes 262176 | tf_op jit(solution)/shard_map/ppermute | solution.py:471
  31.8 0.6 %collective-permute-start.14 = (f32[4,8,8,128]{3,2,1,0:T(8,128)S(1)}, f32[4,8,8,128]{3,2,1,0:T(8,128)S(1)}, u32[]{:S(2)}, u32[]{:S(2)}) collective-permute-start(f32[4,8,8,128]{3,2,1,0:T(8,128)S(1)} %get-tuple-element.64), channel_id=1, source_target_pairs={{0,1},{1,0},{2,3},{3,2},{4,5},{5,4},{6,7},{7,6},{8,9},{9,8},{10,11... | collective-permute-start | bytes 393224 | tf_op jit(solution)/shard_map/ppermute | solution.py:471
  32.4 0.0 collective-permute-done.15.refs_6_.refs_10_
  32.4 0.1 collective-permute-done.16.refs_8_.refs_12_
  32.5 0.4 pull.1.refs_6_.refs_2_
  32.9 0.3 collective-permute-start.20
  33.2 1.0 %collective-permute-start.21 = (f32[2,128,128]{2,1,0:T(8,128)S(1)}, f32[2,128,128]{2,1,0:T(8,128)S(1)}, u32[]{:S(2)}, u32[]{:S(2)}) collective-permute-start(f32[2,128,128]{2,1,0:T(8,128)S(1)} %pull.1.refs_6_.refs_2_), channel_id=1, source_target_pairs={{0,16},{8,24},{16,0},{24,8},{1,17},{9,25},{17,1},{25,9},{2,18},{10... | collective-permute-start | bytes 393224 | tf_op jit(solution)/shard_map/ppermute | solution.py:471
  34.2 0.7 %collective-permute-start.22 = (f32[2,128,128]{2,1,0:T(8,128)S(1)}, f32[2,128,128]{2,1,0:T(8,128)S(1)}, u32[]{:S(2)}, u32[]{:S(2)}) collective-permute-start(f32[2,128,128]{2,1,0:T(8,128)S(1)} %pull.1.refs_6_.refs_2_), channel_id=1, source_target_pairs={{0,24},{8,16},{16,8},{24,0},{1,25},{9,17},{17,9},{25,1},{2,26},{10... | collective-permute-start | bytes 393224 | tf_op jit(solution)/shard_map/ppermute | solution.py:471
  34.8 1.5 %bend.1.refs_2_.refs_6_ = f32[16,64,128]{2,1,0:T(8,128)S(1)} custom-call(f32[56,8,128]{2,1,0:T(8,128)S(1)} %get-tuple-element.43.refs_0_, f32[16,256,128]{2,1,0:T(8,128)S(1)} %get-tuple-element.46.refs_1_, f32[8,16,8,8,128]{4,3,2,1,0:T(8,128)S(1)} %get-tuple-element.65.refs_2_, f32[8,16,8,8,128]{4,3,2,1,0:T(8,128)S(1)} %get-tuple-element.66.refs_3_, ...), custom_call_target="tpu_custom_call" | custom-call | bytes 1048576 | tf_op jit(solution)/shard_map/bend/pallas_call | solution.py:64
  36.3 1.1 %collective-permute-done.14.refs_1_ = f32[4,8,8,128]{3,2,1,0:T(8,128)S(1)} collective-permute-done((f32[4,8,8,128]{3,2,1,0:T(8,128)S(1)}, f32[4,8,8,128]{3,2,1,0:T(8,128)S(1)}, u32[]{:S(2)}, u32[]{:S(2)}) %collective-permute-start.14) | collective-permute-done | bytes 131104 | tf_op jit(solution)/shard_map/ppermute | solution.py:471
  37.4 0.7 %collective-permute-start.17 = (f32[2,8,8,128]{3,2,1,0:T(8,128)S(1)}, f32[2,8,8,128]{3,2,1,0:T(8,128)S(1)}, u32[]{:S(2)}, u32[]{:S(2)}) collective-permute-start(f32[2,8,8,128]{3,2,1,0:T(8,128)S(1)} %get-tuple-element.70), channel_id=1, source_target_pairs={{0,2},{1,3},{2,0},{3,1},{4,6},{5,7},{6,4},{7,5},{8,10},{9,11},{10,... | collective-permute-start | bytes 196616 | tf_op jit(solution)/shard_map/ppermute | solution.py:471
  38.1 3.6 %collective-permute-start.18 = (f32[2,8,8,128]{3,2,1,0:T(8,128)S(1)}, f32[2,8,8,128]{3,2,1,0:T(8,128)S(1)}, u32[]{:S(2)}, u32[]{:S(2)}) collective-permute-start(f32[2,8,8,128]{3,2,1,0:T(8,128)S(1)} %get-tuple-element.71), channel_id=1, source_target_pairs={{0,4},{1,5},{2,6},{3,7},{4,0},{5,1},{6,2},{7,3},{8,12},{9,13},{10,... | collective-permute-start | bytes 196616 | tf_op jit(solution)/shard_map/ppermute | solution.py:471
  41.7 0.0 collective-permute-done.20.refs_3_
  41.7 0.2 collective-permute-start.19
  41.9 5.7 %blend.1 = (f32[16,256,128]{2,1,0:T(8,128)}, f32[8,128]{1,0:T(8,128)S(1)}) custom-call(f32[56,8,128]{2,1,0:T(8,128)S(1)} %get-tuple-element.43.refs_0_, f32[16,256,128]{2,1,0:T(8,128)S(1)} %get-tuple-element.46.refs_1_, f32[2,128,128]{2,1,0:T(8,128)S(1)} %pull.1.refs_6_.refs_2_, f32[2,128,128]{2,1,0:T(8,128)S(1)} %collective-permute-done.20.refs_3_, ...), custom_call_target="tpu_custom_call" | custom-call | flops 2400000000 | bytes 1048576 | tf_op jit(solution)/shard_map/blend/pallas_call | solution.py:64
  47.6 0.2 collective-permute-done.19.refs_3_
  47.8 0.8 %picture.1 = f32[8,8,1024]{2,1,0:T(8,128)} custom-call(f32[2,8,8,128]{3,2,1,0:T(8,128)S(1)} %get-tuple-element.69.refs_0_, f32[2,8,8,128]{3,2,1,0:T(8,128)S(1)} %collective-permute-done.17.refs_1_, f32[2,8,8,128]{3,2,1,0:T(8,128)S(1)} %collective-permute-done.18.refs_2_, f32[2,8,8,128]{3,2,1,0:T(8,128)S(1)} %collective-permute-done.19.refs_3_, ...), custom_call_target="tpu_custom_call" | custom-call | bytes 1048576 | tf_op jit(solution)/shard_map/picture/pallas_call | solution.py:64
  (17 shorter events, 0.2 us)
Async XLA Ops:
  3.9 9.7 %collective-permute-start.6 = (f32[2,8,8,128]{3,2,1,0:T(8,128)S(1)}, f32[2,8,8,128]{3,2,1,0:T(8,128)S(1)}, u32[]{:S(2)}, u32[]{:S(2)}) collective-permute-start(f32[2,8,8,128]{3,2,1,0:T(8,128)S(1)} %get-tuple-element.50), channel_id=1, source_target_pairs={{0,2},{1,3},{2,0},{3,1},{4,6},{5,7},{6,4},{7,5},{8,10},{9,11},{10,... | collective-permute-start | bytes 196616 | tf_op jit(solution)/shard_map/ppermute | solution.py:471
  7.0 7.3 %collective-permute-start.7 = (f32[2,8,8,128]{3,2,1,0:T(8,128)S(1)}, f32[2,8,8,128]{3,2,1,0:T(8,128)S(1)}, u32[]{:S(2)}, u32[]{:S(2)}) collective-permute-start(f32[2,8,8,128]{3,2,1,0:T(8,128)S(1)} %get-tuple-element.51), channel_id=1, source_target_pairs={{0,4},{1,5},{2,6},{3,7},{4,0},{5,1},{6,2},{7,3},{8,12},{9,13},{10,... | collective-permute-start | bytes 196616 | tf_op jit(solution)/shard_map/ppermute | solution.py:471
  9.6 6.1 %collective-permute-start.8 = (f32[2,8,8,128]{3,2,1,0:T(8,128)S(1)}, f32[2,8,8,128]{3,2,1,0:T(8,128)S(1)}, u32[]{:S(2)}, u32[]{:S(2)}) collective-permute-start(f32[2,8,8,128]{3,2,1,0:T(8,128)S(1)} %get-tuple-element.52), channel_id=1, source_target_pairs={{0,6},{1,7},{2,4},{3,5},{4,2},{5,3},{6,0},{7,1},{8,14},{9,15},{10,... | collective-permute-start | bytes 196616 | tf_op jit(solution)/shard_map/ppermute | solution.py:471
  9.6 8.2 %collective-permute-start.1 = (f32[2,128,128]{2,1,0:T(8,128)S(1)}, f32[2,128,128]{2,1,0:T(8,128)S(1)}, u32[]{:S(2)}, u32[]{:S(2)}) collective-permute-start(f32[2,128,128]{2,1,0:T(8,128)S(1)} %get-tuple-element.45), channel_id=1, source_target_pairs={{0,16},{8,24},{16,0},{24,8},{1,17},{9,25},{17,1},{25,9},{2,18},{10... | collective-permute-start | bytes 393224 | tf_op jit(solution)/shard_map/ppermute | solution.py:471
  11.3 6.5 %collective-permute-start.4 = (f32[2,128,128]{2,1,0:T(8,128)S(1)}, f32[2,128,128]{2,1,0:T(8,128)S(1)}, u32[]{:S(2)}, u32[]{:S(2)}) collective-permute-start(f32[2,128,128]{2,1,0:T(8,128)S(1)} %get-tuple-element.44), channel_id=1, source_target_pairs={{0,16},{8,24},{16,0},{24,8},{1,17},{9,25},{17,1},{25,9},{2,18},{10... | collective-permute-start | bytes 393224 | tf_op jit(solution)/shard_map/ppermute | solution.py:471
  15.7 7.0 %collective-permute-start.10 = (f32[8,8,8,128]{3,2,1,0:T(8,128)S(1)}, f32[8,8,8,128]{3,2,1,0:T(8,128)S(1)}, u32[]{:S(2)}, u32[]{:S(2)}) collective-permute-start(f32[8,8,8,128]{3,2,1,0:T(8,128)S(1)} %turn.6.refs_3_.refs_0_), channel_id=1, source_target_pairs={{0,16},{8,24},{16,0},{24,8},{1,17},{9,25},{17,1},{25,9},{2,18},{10... | collective-permute-start | bytes 786440 | tf_op jit(solution)/shard_map/ppermute | solution.py:471
  17.2 3.0 %collective-permute-start.3 = (f32[2,128,128]{2,1,0:T(8,128)S(1)}, f32[2,128,128]{2,1,0:T(8,128)S(1)}, u32[]{:S(2)}, u32[]{:S(2)}) collective-permute-start(f32[2,128,128]{2,1,0:T(8,128)S(1)} %get-tuple-element.45), channel_id=1, source_target_pairs={{0,8},{8,0},{16,24},{24,16},{1,9},{9,1},{17,25},{25,17},{2,10},{10... | collective-permute-start | bytes 393224 | tf_op jit(solution)/shard_map/ppermute | solution.py:471
  17.2 7.1 %collective-permute-start = (f32[2,128,128]{2,1,0:T(8,128)S(1)}, f32[2,128,128]{2,1,0:T(8,128)S(1)}, u32[]{:S(2)}, u32[]{:S(2)}) collective-permute-start(f32[2,128,128]{2,1,0:T(8,128)S(1)} %get-tuple-element.44), channel_id=1, source_target_pairs={{0,8},{8,0},{16,24},{24,16},{1,9},{9,1},{17,25},{25,17},{2,10},{10... | collective-permute-start | bytes 393224 | tf_op jit(solution)/shard_map/ppermute | solution.py:471
  17.7 2.5 %collective-permute-start.5 = (f32[2,128,128]{2,1,0:T(8,128)S(1)}, f32[2,128,128]{2,1,0:T(8,128)S(1)}, u32[]{:S(2)}, u32[]{:S(2)}) collective-permute-start(f32[2,128,128]{2,1,0:T(8,128)S(1)} %collective-permute-done.4.refs_2_), channel_id=1, source_target_pairs={{0,8},{8,0},{16,24},{24,16},{1,9},{9,1},{17,25},{25,17},{2,10},{10... | collective-permute-start | bytes 393224 | tf_op jit(solution)/shard_map/ppermute | solution.py:471
  17.7 6.6 %collective-permute-start.2 = (f32[2,128,128]{2,1,0:T(8,128)S(1)}, f32[2,128,128]{2,1,0:T(8,128)S(1)}, u32[]{:S(2)}, u32[]{:S(2)}) collective-permute-start(f32[2,128,128]{2,1,0:T(8,128)S(1)} %collective-permute-done.1.refs_5_.refs_2_), channel_id=1, source_target_pairs={{0,8},{8,0},{16,24},{24,16},{1,9},{9,1},{17,25},{25,17},{2,10},{10... | collective-permute-start | bytes 393224 | tf_op jit(solution)/shard_map/ppermute | solution.py:471
  20.6 3.7 %collective-permute-start.9 = (f32[8,8,8,128]{3,2,1,0:T(8,128)S(1)}, f32[8,8,8,128]{3,2,1,0:T(8,128)S(1)}, u32[]{:S(2)}, u32[]{:S(2)}) collective-permute-start(f32[8,8,8,128]{3,2,1,0:T(8,128)S(1)} %get-tuple-element.55.refs_4_), channel_id=1, source_target_pairs={{0,8},{8,0},{16,24},{24,16},{1,9},{9,1},{17,25},{25,17},{2,10},{10... | collective-permute-start | bytes 786440 | tf_op jit(solution)/shard_map/ppermute | solution.py:471
  22.7 7.5 %collective-permute-start.13 = (f32[8,8,8,128]{3,2,1,0:T(8,128)S(1)}, f32[8,8,8,128]{3,2,1,0:T(8,128)S(1)}, u32[]{:S(2)}, u32[]{:S(2)}) collective-permute-start(f32[8,8,8,128]{3,2,1,0:T(8,128)S(1)} %get-tuple-element.61), channel_id=1, source_target_pairs={{0,1},{1,0},{2,3},{3,2},{4,5},{5,4},{6,7},{7,6},{8,9},{9,8},{10,11... | collective-permute-start | bytes 786440 | tf_op jit(solution)/shard_map/ppermute | solution.py:471
  24.3 6.6 %collective-permute-start.12 = (f32[8,8,8,128]{3,2,1,0:T(8,128)S(1)}, f32[8,8,8,128]{3,2,1,0:T(8,128)S(1)}, u32[]{:S(2)}, u32[]{:S(2)}) collective-permute-start(f32[8,8,8,128]{3,2,1,0:T(8,128)S(1)} %total.1.refs_3_.refs_4_), channel_id=1, source_target_pairs={{0,16},{8,24},{16,0},{24,8},{1,17},{9,25},{17,1},{25,9},{2,18},{10... | collective-permute-start | bytes 786440 | tf_op jit(solution)/shard_map/ppermute | solution.py:471
  30.2 1.6 %collective-permute-start.11 = (f32[8,8,8,128]{3,2,1,0:T(8,128)S(1)}, f32[8,8,8,128]{3,2,1,0:T(8,128)S(1)}, u32[]{:S(2)}, u32[]{:S(2)}) collective-permute-start(f32[8,8,8,128]{3,2,1,0:T(8,128)S(1)} %get-tuple-element.60.refs_2_), channel_id=1, source_target_pairs={{0,8},{8,0},{16,24},{24,16},{1,9},{9,1},{17,25},{25,17},{2,10},{10... | collective-permute-start | bytes 786440 | tf_op jit(solution)/shard_map/ppermute | solution.py:471
  30.3 2.1 %collective-permute-start.15 = (f32[8,8,8,128]{3,2,1,0:T(8,128)S(1)}, f32[8,8,8,128]{3,2,1,0:T(8,128)S(1)}, u32[]{:S(2)}, u32[]{:S(2)}) collective-permute-start(f32[8,8,8,128]{3,2,1,0:T(8,128)S(1)} %get-tuple-element.62.refs_1_.refs_5_), channel_id=1, source_target_pairs={{0,8},{8,0},{16,24},{24,16},{1,9},{9,1},{17,25},{25,17},{2,10},{10... | collective-permute-start | bytes 786440 | tf_op jit(solution)/shard_map/ppermute | solution.py:471
  30.8 1.7 %collective-permute-start.16 = (f32[8,8,8,128]{3,2,1,0:T(8,128)S(1)}, f32[8,8,8,128]{3,2,1,0:T(8,128)S(1)}, u32[]{:S(2)}, u32[]{:S(2)}) collective-permute-start(f32[8,8,8,128]{3,2,1,0:T(8,128)S(1)} %get-tuple-element.68.refs_7_.refs_11_), channel_id=1, source_target_pairs={{0,8},{8,0},{16,24},{24,16},{1,9},{9,1},{17,25},{25,17},{2,10},{10... | collective-permute-start | bytes 786440 | tf_op jit(solution)/shard_map/ppermute | solution.py:471
  31.8 5.6 %collective-permute-start.14 = (f32[4,8,8,128]{3,2,1,0:T(8,128)S(1)}, f32[4,8,8,128]{3,2,1,0:T(8,128)S(1)}, u32[]{:S(2)}, u32[]{:S(2)}) collective-permute-start(f32[4,8,8,128]{3,2,1,0:T(8,128)S(1)} %get-tuple-element.64), channel_id=1, source_target_pairs={{0,1},{1,0},{2,3},{3,2},{4,5},{5,4},{6,7},{7,6},{8,9},{9,8},{10,11... | collective-permute-start | bytes 393224 | tf_op jit(solution)/shard_map/ppermute | solution.py:471
  32.9 8.8 %collective-permute-start.20 = (f32[2,128,128]{2,1,0:T(8,128)S(1)}, f32[2,128,128]{2,1,0:T(8,128)S(1)}, u32[]{:S(2)}, u32[]{:S(2)}) collective-permute-start(f32[2,128,128]{2,1,0:T(8,128)S(1)} %pull.1.refs_6_.refs_2_), channel_id=1, source_target_pairs={{0,8},{8,0},{16,24},{24,16},{1,9},{9,1},{17,25},{25,17},{2,10},{10... | collective-permute-start | bytes 393224 | tf_op jit(solution)/shard_map/ppermute | solution.py:471
  33.2 8.7 %collective-permute-start.21 = (f32[2,128,128]{2,1,0:T(8,128)S(1)}, f32[2,128,128]{2,1,0:T(8,128)S(1)}, u32[]{:S(2)}, u32[]{:S(2)}) collective-permute-start(f32[2,128,128]{2,1,0:T(8,128)S(1)} %pull.1.refs_6_.refs_2_), channel_id=1, source_target_pairs={{0,16},{8,24},{16,0},{24,8},{1,17},{9,25},{17,1},{25,9},{2,18},{10... | collective-permute-start | bytes 393224 | tf_op jit(solution)/shard_map/ppermute | solution.py:471
  34.2 7.7 %collective-permute-start.22 = (f32[2,128,128]{2,1,0:T(8,128)S(1)}, f32[2,128,128]{2,1,0:T(8,128)S(1)}, u32[]{:S(2)}, u32[]{:S(2)}) collective-permute-start(f32[2,128,128]{2,1,0:T(8,128)S(1)} %pull.1.refs_6_.refs_2_), channel_id=1, source_target_pairs={{0,24},{8,16},{16,8},{24,0},{1,25},{9,17},{17,9},{25,1},{2,26},{10... | collective-permute-start | bytes 393224 | tf_op jit(solution)/shard_map/ppermute | solution.py:471
  37.4 10.1 %collective-permute-start.17 = (f32[2,8,8,128]{3,2,1,0:T(8,128)S(1)}, f32[2,8,8,128]{3,2,1,0:T(8,128)S(1)}, u32[]{:S(2)}, u32[]{:S(2)}) collective-permute-start(f32[2,8,8,128]{3,2,1,0:T(8,128)S(1)} %get-tuple-element.70), channel_id=1, source_target_pairs={{0,2},{1,3},{2,0},{3,1},{4,6},{5,7},{6,4},{7,5},{8,10},{9,11},{10,... | collective-permute-start | bytes 196616 | tf_op jit(solution)/shard_map/ppermute | solution.py:471
  38.1 9.5 %collective-permute-start.18 = (f32[2,8,8,128]{3,2,1,0:T(8,128)S(1)}, f32[2,8,8,128]{3,2,1,0:T(8,128)S(1)}, u32[]{:S(2)}, u32[]{:S(2)}) collective-permute-start(f32[2,8,8,128]{3,2,1,0:T(8,128)S(1)} %get-tuple-element.71), channel_id=1, source_target_pairs={{0,4},{1,5},{2,6},{3,7},{4,0},{5,1},{6,2},{7,3},{8,12},{9,13},{10,... | collective-permute-start | bytes 196616 | tf_op jit(solution)/shard_map/ppermute | solution.py:471
  41.7 6.1 %collective-permute-start.19 = (f32[2,8,8,128]{3,2,1,0:T(8,128)S(1)}, f32[2,8,8,128]{3,2,1,0:T(8,128)S(1)}, u32[]{:S(2)}, u32[]{:S(2)}) collective-permute-start(f32[2,8,8,128]{3,2,1,0:T(8,128)S(1)} %get-tuple-element.72), channel_id=1, source_target_pairs={{0,6},{1,7},{2,4},{3,5},{4,2},{5,3},{6,0},{7,1},{8,14},{9,15},{10,... | collective-permute-start | bytes 196616 | tf_op jit(solution)/shard_map/ppermute | solution.py:471

commit v3 on v2

--- a/solution.py
+++ b/solution.py
@@ -173,9 +173,14 @@
                 heat = thermal_ref[k, here]
                 soot = soot_ref[k, here].astype(F32)
                 cold = pltpu.reciprocal(heat, approx=True)
+                glow = []
+                for b in range(0, bands, 2):
+                    x, y = (jnp.exp2(cold * const(PLANCK_STEP, b + i)) - 1.0 for i in range(2))
+                    inverse = pltpu.reciprocal(x * y, approx=True)
+                    glow += [y * inverse, x * inverse]
                 for b in range(bands):
                     fade = jnp.exp2(soot * const(SOOT_STEP, b) + heat * const(GAS_STEP, b))
-                    source = pltpu.reciprocal(jnp.exp2(cold * const(PLANCK_STEP, b)) - 1.0, approx=True)
+                    source = glow[b]
                     fade_ref[2 * i, k, b] = fade[:ROWS]
                     fade_ref[2 * i + 1, k, b] = fade[ROWS:]
                     source_ref[2 * i, k, b] = source[:ROWS]

time: 48.8 us -> 48.8 us (level)
  no operation moved by 1% of the time
where the time goes in v3:
time: 48.8 us; the launch traced here: 48.7 us
  starting transfers between devices  21.2 us (43%)
  Pallas kernels  20.4 us (42%)
  waiting for transfers between devices  6.22 us (13%)
  between operations  0.81 us (2%)
    ppermute x23, starting transfers between devices, swap(): return lax.ppermute(value, axis, pairs)  21.2 us
    pallas_call x19, Pallas kernels, run(): call(*[pltpu.with_memory_space_constraint(x, pltpu.VMEM) if held(spec) el...  20.4 us
    ppermute x23, waiting for transfers between devices, swap(): return lax.ppermute(value, axis, pairs)  6.22 us
  transfers between devices with their start and end apart: 23, of which 7 were waited for; matrix products, arithmetic and copies ran while one was open for 0% of the time, Pallas kernels for 34%

profile of v3, /device:TPU:0, one launch (start us, length us, event | category | flops | bytes accessed | tf_op | source)
XLA Modules:
  0.0 48.7 jit_solution(7270904262838321659)
XLA Ops:
  0.6 3.2 %load.1 = (f32[16,256,128]{2,1,0:T(8,128)S(1)}, bf16[16,256,128]{2,1,0:T(8,128)(2,1)S(1)}, f32[2,128,128]{2,1,0:T(8,128)S(1)}, f32[2,128,128]{2,1,0:T(8,128)S(1)...) custom-call(f32[8]{0:T(128)} %refs_0_.1, ...), custom_call_target="tpu_custom_call" | custom-call | bytes 1048576 | tf_op jit(solution)/shard_map/load/pallas_call | solution.py:64
  3.9 3.1 %collective-permute-start.6 = (f32[2,8,8,128]{3,2,1,0:T(8,128)S(1)}, f32[2,8,8,128]{3,2,1,0:T(8,128)S(1)}, u32[]{:S(2)}, u32[]{:S(2)}) collective-permute-start(f32[2,8,8,128]{3,2,1,0:T(8,128)S(1)} %get-tuple-element.50), channel_id=1, source_target_pairs={{0,2},{1,3},{2,0},{3,1},{4,6},{5,7},{6,4},{7,5},{8,10},{9,11},{10,... | collective-permute-start | bytes 196616 | tf_op jit(solution)/shard_map/ppermute | solution.py:476
  7.0 2.6 %collective-permute-start.7 = (f32[2,8,8,128]{3,2,1,0:T(8,128)S(1)}, f32[2,8,8,128]{3,2,1,0:T(8,128)S(1)}, u32[]{:S(2)}, u32[]{:S(2)}) collective-permute-start(f32[2,8,8,128]{3,2,1,0:T(8,128)S(1)} %get-tuple-element.51), channel_id=1, source_target_pairs={{0,4},{1,5},{2,6},{3,7},{4,0},{5,1},{6,2},{7,3},{8,12},{9,13},{10,... | collective-permute-start | bytes 196616 | tf_op jit(solution)/shard_map/ppermute | solution.py:476
  9.6 1.7 %collective-permute-start.1 = (f32[2,128,128]{2,1,0:T(8,128)S(1)}, f32[2,128,128]{2,1,0:T(8,128)S(1)}, u32[]{:S(2)}, u32[]{:S(2)}) collective-permute-start(f32[2,128,128]{2,1,0:T(8,128)S(1)} %get-tuple-element.45), channel_id=1, source_target_pairs={{0,16},{8,24},{16,0},{24,8},{1,17},{9,25},{17,1},{25,9},{2,18},{10... | collective-permute-start | bytes 393224 | tf_op jit(solution)/shard_map/ppermute | solution.py:476
  11.3 0.3 collective-permute-start.4
  11.6 2.0 %march.4 = (f32[8,16,8,8,128]{4,3,2,1,0:T(8,128)S(1)}, f32[8,16,8,8,128]{4,3,2,1,0:T(8,128)S(1)}, f32[8,8,8,128]{3,2,1,0:T(8,128)S(1)}) custom-call(f32[56,8,128]{2,1,0:T(8,128)S(1)} %get-tuple-element.43.refs_0_, f32[16,256,128]{2,1,0:T(8,128)S(1)} %get-tuple-element.46.refs_1_, bf16[16,256,128]{2,1,0:T(8,128)(2,1)S(1)} %get-tuple-element.47.refs_2_), custom_call_target="tpu_custom_call" | custom-call | flops 2400000000 | bytes 1048576 | tf_op jit(solution)/shard_map/march/pallas_call | solution.py:64
  13.6 0.0 collective-permute-done.6.refs_1_
  13.6 0.7 %collective-permute-done.7.refs_2_ = f32[2,8,8,128]{3,2,1,0:T(8,128)S(1)} collective-permute-done((f32[2,8,8,128]{3,2,1,0:T(8,128)S(1)}, f32[2,8,8,128]{3,2,1,0:T(8,128)S(1)}, u32[]{:S(2)}, u32[]{:S(2)}) %collective-permute-start.7) | collective-permute-done | bytes 65568 | tf_op jit(solution)/shard_map/ppermute | solution.py:476
  14.2 1.4 %collective-permute-done.8.refs_3_ = f32[2,8,8,128]{3,2,1,0:T(8,128)S(1)} collective-permute-done((f32[2,8,8,128]{3,2,1,0:T(8,128)S(1)}, f32[2,8,8,128]{3,2,1,0:T(8,128)S(1)}, u32[]{:S(2)}, u32[]{:S(2)}) %collective-permute-start.8) | collective-permute-done | bytes 65568 | tf_op jit(solution)/shard_map/ppermute | solution.py:476
  15.7 1.6 %collective-permute-start.10 = (f32[8,8,8,128]{3,2,1,0:T(8,128)S(1)}, f32[8,8,8,128]{3,2,1,0:T(8,128)S(1)}, u32[]{:S(2)}, u32[]{:S(2)}) collective-permute-start(f32[8,8,8,128]{3,2,1,0:T(8,128)S(1)} %turn.6.refs_3_.refs_0_), channel_id=1, source_target_pairs={{0,16},{8,24},{16,0},{24,8},{1,17},{9,25},{17,1},{25,9},{2,18},{10... | collective-permute-start | bytes 786440 | tf_op jit(solution)/shard_map/ppermute | solution.py:476
  17.2 0.0 collective-permute-start.3
  17.2 0.5 %collective-permute-start = (f32[2,128,128]{2,1,0:T(8,128)S(1)}, f32[2,128,128]{2,1,0:T(8,128)S(1)}, u32[]{:S(2)}, u32[]{:S(2)}) collective-permute-start(f32[2,128,128]{2,1,0:T(8,128)S(1)} %get-tuple-element.44), channel_id=1, source_target_pairs={{0,8},{8,0},{16,24},{24,16},{1,9},{9,1},{17,25},{25,17},{2,10},{10... | collective-permute-start | bytes 393224 | tf_op jit(solution)/shard_map/ppermute | solution.py:476
  17.7 0.0 collective-permute-start.5
  17.7 0.0 collective-permute-done.1.refs_5_.refs_2_
  17.7 0.5 %collective-permute-start.2 = (f32[2,128,128]{2,1,0:T(8,128)S(1)}, f32[2,128,128]{2,1,0:T(8,128)S(1)}, u32[]{:S(2)}, u32[]{:S(2)}) collective-permute-start(f32[2,128,128]{2,1,0:T(8,128)S(1)} %collective-permute-done.1.refs_5_.refs_2_), channel_id=1, source_target_pairs={{0,8},{8,0},{16,24},{24,16},{1,9},{9,1},{17,25},{25,17},{2,10},{10... | collective-permute-start | bytes 393224 | tf_op jit(solution)/shard_map/ppermute | solution.py:476
  18.2 2.0 %march.5 = (f32[8,16,8,8,128]{4,3,2,1,0:T(8,128)S(1)}, f32[8,16,8,8,128]{4,3,2,1,0:T(8,128)S(1)}, f32[8,8,8,128]{3,2,1,0:T(8,128)S(1)}) custom-call(f32[56,8,128]{2,1,0:T(8,128)S(1)} %get-tuple-element.43.refs_0_, f32[16,256,128]{2,1,0:T(8,128)S(1)} %get-tuple-element.46.refs_1_, bf16[16,256,128]{2,1,0:T(8,128)(2,1)S(1)} %get-tuple-element.47.refs_2_, ...), custom_call_target="tpu_custom_call" | custom-call | flops 2400000000 | bytes 1048576 | tf_op jit(solution)/shard_map/march/pallas_call | solution.py:64
  20.2 0.0 collective-permute-done.3.refs_1_
  20.2 0.4 dim.2
  20.6 0.1 collective-permute-start.9
  20.8 1.9 %collective-permute-done.10.refs_1_ = f32[8,8,8,128]{3,2,1,0:T(8,128)S(1)} collective-permute-done((f32[8,8,8,128]{3,2,1,0:T(8,128)S(1)}, f32[8,8,8,128]{3,2,1,0:T(8,128)S(1)}, u32[]{:S(2)}, u32[]{:S(2)}) %collective-permute-start.10) | collective-permute-done | bytes 262176 | tf_op jit(solution)/shard_map/ppermute | solution.py:476
  22.7 1.6 %collective-permute-start.13 = (f32[8,8,8,128]{3,2,1,0:T(8,128)S(1)}, f32[8,8,8,128]{3,2,1,0:T(8,128)S(1)}, u32[]{:S(2)}, u32[]{:S(2)}) collective-permute-start(f32[8,8,8,128]{3,2,1,0:T(8,128)S(1)} %get-tuple-element.61), channel_id=1, source_target_pairs={{0,1},{1,0},{2,3},{3,2},{4,5},{5,4},{6,7},{7,6},{8,9},{9,8},{10,11... | collective-permute-start | bytes 786440 | tf_op jit(solution)/shard_map/ppermute | solution.py:476
  24.3 0.0 collective-permute-done.refs_3_.refs_1_
  24.3 0.0 collective-permute-done.2.refs_4_.refs_3_
  24.3 0.0 collective-permute-done.9.refs_1_
  24.3 1.6 %collective-permute-start.12 = (f32[8,8,8,128]{3,2,1,0:T(8,128)S(1)}, f32[8,8,8,128]{3,2,1,0:T(8,128)S(1)}, u32[]{:S(2)}, u32[]{:S(2)}) collective-permute-start(f32[8,8,8,128]{3,2,1,0:T(8,128)S(1)} %total.1.refs_3_.refs_4_), channel_id=1, source_target_pairs={{0,16},{8,24},{16,0},{24,8},{1,17},{9,25},{17,1},{25,9},{2,18},{10... | collective-permute-start | bytes 786440 | tf_op jit(solution)/shard_map/ppermute | solution.py:476
  25.9 2.0 %march.6 = (f32[8,16,8,8,128]{4,3,2,1,0:T(8,128)S(1)}, f32[8,16,8,8,128]{4,3,2,1,0:T(8,128)S(1)}, f32[8,8,8,128]{3,2,1,0:T(8,128)S(1)}) custom-call(f32[56,8,128]{2,1,0:T(8,128)S(1)} %get-tuple-element.43.refs_0_, f32[16,256,128]{2,1,0:T(8,128)S(1)} %get-tuple-element.46.refs_1_, bf16[16,256,128]{2,1,0:T(8,128)(2,1)S(1)} %get-tuple-element.47.refs_2_, ...), custom_call_target="tpu_custom_call" | custom-call | flops 100000000 | bytes 1048576 | tf_op jit(solution)/shard_map/march/pallas_call | solution.py:64
  27.9 2.0 %march.7 = (f32[8,16,8,8,128]{4,3,2,1,0:T(8,128)S(1)}, f32[8,16,8,8,128]{4,3,2,1,0:T(8,128)S(1)}, f32[8,8,8,128]{3,2,1,0:T(8,128)S(1)}) custom-call(f32[56,8,128]{2,1,0:T(8,128)S(1)} %get-tuple-element.43.refs_0_, f32[16,256,128]{2,1,0:T(8,128)S(1)} %get-tuple-element.46.refs_1_, bf16[16,256,128]{2,1,0:T(8,128)(2,1)S(1)} %get-tuple-element.47.refs_2_, ...), custom_call_target="tpu_custom_call" | custom-call | flops 100000000 | bytes 1048576 | tf_op jit(solution)/shard_map/march/pallas_call | solution.py:64
  29.9 0.4 dim.3
  30.3 0.1 collective-permute-start.11
  30.3 0.0 collective-permute-done.13.refs_1_
  30.4 0.5 %collective-permute-start.15 = (f32[8,8,8,128]{3,2,1,0:T(8,128)S(1)}, f32[8,8,8,128]{3,2,1,0:T(8,128)S(1)}, u32[]{:S(2)}, u32[]{:S(2)}) collective-permute-start(f32[8,8,8,128]{3,2,1,0:T(8,128)S(1)} %get-tuple-element.62.refs_1_.refs_5_), channel_id=1, source_target_pairs={{0,8},{8,0},{16,24},{24,16},{1,9},{9,1},{17,25},{25,17},{2,10},{10... | collective-permute-start | bytes 786440 | tf_op jit(solution)/shard_map/ppermute | solution.py:476
  31.0 0.1 collective-permute-start.16
  31.0 0.0 collective-permute-done.12.refs_0_
  31.1 0.8 %collective-permute-done.11.refs_1_ = f32[8,8,8,128]{3,2,1,0:T(8,128)S(1)} collective-permute-done((f32[8,8,8,128]{3,2,1,0:T(8,128)S(1)}, f32[8,8,8,128]{3,2,1,0:T(8,128)S(1)}, u32[]{:S(2)}, u32[]{:S(2)}) %collective-permute-start.11) | collective-permute-done | bytes 262176 | tf_op jit(solution)/shard_map/ppermute | solution.py:476
  31.9 0.6 %collective-permute-start.14 = (f32[4,8,8,128]{3,2,1,0:T(8,128)S(1)}, f32[4,8,8,128]{3,2,1,0:T(8,128)S(1)}, u32[]{:S(2)}, u32[]{:S(2)}) collective-permute-start(f32[4,8,8,128]{3,2,1,0:T(8,128)S(1)} %get-tuple-element.64), channel_id=1, source_target_pairs={{0,1},{1,0},{2,3},{3,2},{4,5},{5,4},{6,7},{7,6},{8,9},{9,8},{10,11... | collective-permute-start | bytes 393224 | tf_op jit(solution)/shard_map/ppermute | solution.py:476
  32.5 0.1 collective-permute-done.16.refs_8_.refs_12_
  32.6 0.4 pull.1.refs_6_.refs_2_
  33.0 0.3 collective-permute-start.20
  33.3 0.9 %collective-permute-start.21 = (f32[2,128,128]{2,1,0:T(8,128)S(1)}, f32[2,128,128]{2,1,0:T(8,128)S(1)}, u32[]{:S(2)}, u32[]{:S(2)}) collective-permute-start(f32[2,128,128]{2,1,0:T(8,128)S(1)} %pull.1.refs_6_.refs_2_), channel_id=1, source_target_pairs={{0,16},{8,24},{16,0},{24,8},{1,17},{9,25},{17,1},{25,9},{2,18},{10... | collective-permute-start | bytes 393224 | tf_op jit(solution)/shard_map/ppermute | solution.py:476
  34.2 0.7 %collective-permute-start.22 = (f32[2,128,128]{2,1,0:T(8,128)S(1)}, f32[2,128,128]{2,1,0:T(8,128)S(1)}, u32[]{:S(2)}, u32[]{:S(2)}) collective-permute-start(f32[2,128,128]{2,1,0:T(8,128)S(1)} %pull.1.refs_6_.refs_2_), channel_id=1, source_target_pairs={{0,24},{8,16},{16,8},{24,0},{1,25},{9,17},{17,9},{25,1},{2,26},{10... | collective-permute-start | bytes 393224 | tf_op jit(solution)/shard_map/ppermute | solution.py:476
  34.9 1.5 %bend.1.refs_2_.refs_6_ = f32[16,64,128]{2,1,0:T(8,128)S(1)} custom-call(f32[56,8,128]{2,1,0:T(8,128)S(1)} %get-tuple-element.43.refs_0_, f32[16,256,128]{2,1,0:T(8,128)S(1)} %get-tuple-element.46.refs_1_, f32[8,16,8,8,128]{4,3,2,1,0:T(8,128)S(1)} %get-tuple-element.65.refs_2_, f32[8,16,8,8,128]{4,3,2,1,0:T(8,128)S(1)} %get-tuple-element.66.refs_3_, ...), custom_call_target="tpu_custom_call" | custom-call | bytes 1048576 | tf_op jit(solution)/shard_map/bend/pallas_call | solution.py:64
  36.4 1.1 %collective-permute-done.14.refs_1_ = f32[4,8,8,128]{3,2,1,0:T(8,128)S(1)} collective-permute-done((f32[4,8,8,128]{3,2,1,0:T(8,128)S(1)}, f32[4,8,8,128]{3,2,1,0:T(8,128)S(1)}, u32[]{:S(2)}, u32[]{:S(2)}) %collective-permute-start.14) | collective-permute-done | bytes 131104 | tf_op jit(solution)/shard_map/ppermute | solution.py:476
  37.5 0.7 %collective-permute-start.17 = (f32[2,8,8,128]{3,2,1,0:T(8,128)S(1)}, f32[2,8,8,128]{3,2,1,0:T(8,128)S(1)}, u32[]{:S(2)}, u32[]{:S(2)}) collective-permute-start(f32[2,8,8,128]{3,2,1,0:T(8,128)S(1)} %get-tuple-element.70), channel_id=1, source_target_pairs={{0,2},{1,3},{2,0},{3,1},{4,6},{5,7},{6,4},{7,5},{8,10},{9,11},{10,... | collective-permute-start | bytes 196616 | tf_op jit(solution)/shard_map/ppermute | solution.py:476
  38.2 3.6 %collective-permute-start.18 = (f32[2,8,8,128]{3,2,1,0:T(8,128)S(1)}, f32[2,8,8,128]{3,2,1,0:T(8,128)S(1)}, u32[]{:S(2)}, u32[]{:S(2)}) collective-permute-start(f32[2,8,8,128]{3,2,1,0:T(8,128)S(1)} %get-tuple-element.71), channel_id=1, source_target_pairs={{0,4},{1,5},{2,6},{3,7},{4,0},{5,1},{6,2},{7,3},{8,12},{9,13},{10,... | collective-permute-start | bytes 196616 | tf_op jit(solution)/shard_map/ppermute | solution.py:476
  41.8 0.2 collective-permute-start.19
  42.0 5.7 %blend.1 = (f32[16,256,128]{2,1,0:T(8,128)}, f32[8,128]{1,0:T(8,128)S(1)}) custom-call(f32[56,8,128]{2,1,0:T(8,128)S(1)} %get-tuple-element.43.refs_0_, f32[16,256,128]{2,1,0:T(8,128)S(1)} %get-tuple-element.46.refs_1_, f32[2,128,128]{2,1,0:T(8,128)S(1)} %pull.1.refs_6_.refs_2_, f32[2,128,128]{2,1,0:T(8,128)S(1)} %collective-permute-done.20.refs_3_, ...), custom_call_target="tpu_custom_call" | custom-call | flops 2400000000 | bytes 1048576 | tf_op jit(solution)/shard_map/blend/pallas_call | solution.py:64
  47.7 0.2 collective-permute-done.19.refs_3_
  47.9 0.8 %picture.1 = f32[8,8,1024]{2,1,0:T(8,128)} custom-call(f32[2,8,8,128]{3,2,1,0:T(8,128)S(1)} %get-tuple-element.69.refs_0_, f32[2,8,8,128]{3,2,1,0:T(8,128)S(1)} %collective-permute-done.17.refs_1_, f32[2,8,8,128]{3,2,1,0:T(8,128)S(1)} %collective-permute-done.18.refs_2_, f32[2,8,8,128]{3,2,1,0:T(8,128)S(1)} %collective-permute-done.19.refs_3_, ...), custom_call_target="tpu_custom_call" | custom-call | bytes 1048576 | tf_op jit(solution)/shard_map/picture/pallas_call | solution.py:64
  (17 shorter events, 0.2 us)
Async XLA Ops:
  3.9 9.7 %collective-permute-start.6 = (f32[2,8,8,128]{3,2,1,0:T(8,128)S(1)}, f32[2,8,8,128]{3,2,1,0:T(8,128)S(1)}, u32[]{:S(2)}, u32[]{:S(2)}) collective-permute-start(f32[2,8,8,128]{3,2,1,0:T(8,128)S(1)} %get-tuple-element.50), channel_id=1, source_target_pairs={{0,2},{1,3},{2,0},{3,1},{4,6},{5,7},{6,4},{7,5},{8,10},{9,11},{10,... | collective-permute-start | bytes 196616 | tf_op jit(solution)/shard_map/ppermute | solution.py:476
  7.0 7.3 %collective-permute-start.7 = (f32[2,8,8,128]{3,2,1,0:T(8,128)S(1)}, f32[2,8,8,128]{3,2,1,0:T(8,128)S(1)}, u32[]{:S(2)}, u32[]{:S(2)}) collective-permute-start(f32[2,8,8,128]{3,2,1,0:T(8,128)S(1)} %get-tuple-element.51), channel_id=1, source_target_pairs={{0,4},{1,5},{2,6},{3,7},{4,0},{5,1},{6,2},{7,3},{8,12},{9,13},{10,... | collective-permute-start | bytes 196616 | tf_op jit(solution)/shard_map/ppermute | solution.py:476
  9.6 6.1 %collective-permute-start.8 = (f32[2,8,8,128]{3,2,1,0:T(8,128)S(1)}, f32[2,8,8,128]{3,2,1,0:T(8,128)S(1)}, u32[]{:S(2)}, u32[]{:S(2)}) collective-permute-start(f32[2,8,8,128]{3,2,1,0:T(8,128)S(1)} %get-tuple-element.52), channel_id=1, source_target_pairs={{0,6},{1,7},{2,4},{3,5},{4,2},{5,3},{6,0},{7,1},{8,14},{9,15},{10,... | collective-permute-start | bytes 196616 | tf_op jit(solution)/shard_map/ppermute | solution.py:476
  9.6 8.2 %collective-permute-start.1 = (f32[2,128,128]{2,1,0:T(8,128)S(1)}, f32[2,128,128]{2,1,0:T(8,128)S(1)}, u32[]{:S(2)}, u32[]{:S(2)}) collective-permute-start(f32[2,128,128]{2,1,0:T(8,128)S(1)} %get-tuple-element.45), channel_id=1, source_target_pairs={{0,16},{8,24},{16,0},{24,8},{1,17},{9,25},{17,1},{25,9},{2,18},{10... | collective-permute-start | bytes 393224 | tf_op jit(solution)/shard_map/ppermute | solution.py:476
  11.3 6.5 %collective-permute-start.4 = (f32[2,128,128]{2,1,0:T(8,128)S(1)}, f32[2,128,128]{2,1,0:T(8,128)S(1)}, u32[]{:S(2)}, u32[]{:S(2)}) collective-permute-start(f32[2,128,128]{2,1,0:T(8,128)S(1)} %get-tuple-element.44), channel_id=1, source_target_pairs={{0,16},{8,24},{16,0},{24,8},{1,17},{9,25},{17,1},{25,9},{2,18},{10... | collective-permute-start | bytes 393224 | tf_op jit(solution)/shard_map/ppermute | solution.py:476
  15.7 7.0 %collective-permute-start.10 = (f32[8,8,8,128]{3,2,1,0:T(8,128)S(1)}, f32[8,8,8,128]{3,2,1,0:T(8,128)S(1)}, u32[]{:S(2)}, u32[]{:S(2)}) collective-permute-start(f32[8,8,8,128]{3,2,1,0:T(8,128)S(1)} %turn.6.refs_3_.refs_0_), channel_id=1, source_target_pairs={{0,16},{8,24},{16,0},{24,8},{1,17},{9,25},{17,1},{25,9},{2,18},{10... | collective-permute-start | bytes 786440 | tf_op jit(solution)/shard_map/ppermute | solution.py:476
  17.2 3.0 %collective-permute-start.3 = (f32[2,128,128]{2,1,0:T(8,128)S(1)}, f32[2,128,128]{2,1,0:T(8,128)S(1)}, u32[]{:S(2)}, u32[]{:S(2)}) collective-permute-start(f32[2,128,128]{2,1,0:T(8,128)S(1)} %get-tuple-element.45), channel_id=1, source_target_pairs={{0,8},{8,0},{16,24},{24,16},{1,9},{9,1},{17,25},{25,17},{2,10},{10... | collective-permute-start | bytes 393224 | tf_op jit(solution)/shard_map/ppermute | solution.py:476
  17.2 7.1 %collective-permute-start = (f32[2,128,128]{2,1,0:T(8,128)S(1)}, f32[2,128,128]{2,1,0:T(8,128)S(1)}, u32[]{:S(2)}, u32[]{:S(2)}) collective-permute-start(f32[2,128,128]{2,1,0:T(8,128)S(1)} %get-tuple-element.44), channel_id=1, source_target_pairs={{0,8},{8,0},{16,24},{24,16},{1,9},{9,1},{17,25},{25,17},{2,10},{10... | collective-permute-start | bytes 393224 | tf_op jit(solution)/shard_map/ppermute | solution.py:476
  17.7 2.5 %collective-permute-start.5 = (f32[2,128,128]{2,1,0:T(8,128)S(1)}, f32[2,128,128]{2,1,0:T(8,128)S(1)}, u32[]{:S(2)}, u32[]{:S(2)}) collective-permute-start(f32[2,128,128]{2,1,0:T(8,128)S(1)} %collective-permute-done.4.refs_2_), channel_id=1, source_target_pairs={{0,8},{8,0},{16,24},{24,16},{1,9},{9,1},{17,25},{25,17},{2,10},{10... | collective-permute-start | bytes 393224 | tf_op jit(solution)/shard_map/ppermute | solution.py:476
  17.7 6.6 %collective-permute-start.2 = (f32[2,128,128]{2,1,0:T(8,128)S(1)}, f32[2,128,128]{2,1,0:T(8,128)S(1)}, u32[]{:S(2)}, u32[]{:S(2)}) collective-permute-start(f32[2,128,128]{2,1,0:T(8,128)S(1)} %collective-permute-done.1.refs_5_.refs_2_), channel_id=1, source_target_pairs={{0,8},{8,0},{16,24},{24,16},{1,9},{9,1},{17,25},{25,17},{2,10},{10... | collective-permute-start | bytes 393224 | tf_op jit(solution)/shard_map/ppermute | solution.py:476
  20.6 3.7 %collective-permute-start.9 = (f32[8,8,8,128]{3,2,1,0:T(8,128)S(1)}, f32[8,8,8,128]{3,2,1,0:T(8,128)S(1)}, u32[]{:S(2)}, u32[]{:S(2)}) collective-permute-start(f32[8,8,8,128]{3,2,1,0:T(8,128)S(1)} %get-tuple-element.55.refs_4_), channel_id=1, source_target_pairs={{0,8},{8,0},{16,24},{24,16},{1,9},{9,1},{17,25},{25,17},{2,10},{10... | collective-permute-start | bytes 786440 | tf_op jit(solution)/shard_map/ppermute | solution.py:476
  22.7 7.6 %collective-permute-start.13 = (f32[8,8,8,128]{3,2,1,0:T(8,128)S(1)}, f32[8,8,8,128]{3,2,1,0:T(8,128)S(1)}, u32[]{:S(2)}, u32[]{:S(2)}) collective-permute-start(f32[8,8,8,128]{3,2,1,0:T(8,128)S(1)} %get-tuple-element.61), channel_id=1, source_target_pairs={{0,1},{1,0},{2,3},{3,2},{4,5},{5,4},{6,7},{7,6},{8,9},{9,8},{10,11... | collective-permute-start | bytes 786440 | tf_op jit(solution)/shard_map/ppermute | solution.py:476
  24.3 6.7 %collective-permute-start.12 = (f32[8,8,8,128]{3,2,1,0:T(8,128)S(1)}, f32[8,8,8,128]{3,2,1,0:T(8,128)S(1)}, u32[]{:S(2)}, u32[]{:S(2)}) collective-permute-start(f32[8,8,8,128]{3,2,1,0:T(8,128)S(1)} %total.1.refs_3_.refs_4_), channel_id=1, source_target_pairs={{0,16},{8,24},{16,0},{24,8},{1,17},{9,25},{17,1},{25,9},{2,18},{10... | collective-permute-start | bytes 786440 | tf_op jit(solution)/shard_map/ppermute | solution.py:476
  30.3 1.6 %collective-permute-start.11 = (f32[8,8,8,128]{3,2,1,0:T(8,128)S(1)}, f32[8,8,8,128]{3,2,1,0:T(8,128)S(1)}, u32[]{:S(2)}, u32[]{:S(2)}) collective-permute-start(f32[8,8,8,128]{3,2,1,0:T(8,128)S(1)} %get-tuple-element.60.refs_2_), channel_id=1, source_target_pairs={{0,8},{8,0},{16,24},{24,16},{1,9},{9,1},{17,25},{25,17},{2,10},{10... | collective-permute-start | bytes 786440 | tf_op jit(solution)/shard_map/ppermute | solution.py:476
  30.4 2.1 %collective-permute-start.15 = (f32[8,8,8,128]{3,2,1,0:T(8,128)S(1)}, f32[8,8,8,128]{3,2,1,0:T(8,128)S(1)}, u32[]{:S(2)}, u32[]{:S(2)}) collective-permute-start(f32[8,8,8,128]{3,2,1,0:T(8,128)S(1)} %get-tuple-element.62.refs_1_.refs_5_), channel_id=1, source_target_pairs={{0,8},{8,0},{16,24},{24,16},{1,9},{9,1},{17,25},{25,17},{2,10},{10... | collective-permute-start | bytes 786440 | tf_op jit(solution)/shard_map/ppermute | solution.py:476
  31.0 1.7 %collective-permute-start.16 = (f32[8,8,8,128]{3,2,1,0:T(8,128)S(1)}, f32[8,8,8,128]{3,2,1,0:T(8,128)S(1)}, u32[]{:S(2)}, u32[]{:S(2)}) collective-permute-start(f32[8,8,8,128]{3,2,1,0:T(8,128)S(1)} %get-tuple-element.68.refs_7_.refs_11_), channel_id=1, source_target_pairs={{0,8},{8,0},{16,24},{24,16},{1,9},{9,1},{17,25},{25,17},{2,10},{10... | collective-permute-start | bytes 786440 | tf_op jit(solution)/shard_map/ppermute | solution.py:476
  31.9 5.6 %collective-permute-start.14 = (f32[4,8,8,128]{3,2,1,0:T(8,128)S(1)}, f32[4,8,8,128]{3,2,1,0:T(8,128)S(1)}, u32[]{:S(2)}, u32[]{:S(2)}) collective-permute-start(f32[4,8,8,128]{3,2,1,0:T(8,128)S(1)} %get-tuple-element.64), channel_id=1, source_target_pairs={{0,1},{1,0},{2,3},{3,2},{4,5},{5,4},{6,7},{7,6},{8,9},{9,8},{10,11... | collective-permute-start | bytes 393224 | tf_op jit(solution)/shard_map/ppermute | solution.py:476
  33.0 8.8 %collective-permute-start.20 = (f32[2,128,128]{2,1,0:T(8,128)S(1)}, f32[2,128,128]{2,1,0:T(8,128)S(1)}, u32[]{:S(2)}, u32[]{:S(2)}) collective-permute-start(f32[2,128,128]{2,1,0:T(8,128)S(1)} %pull.1.refs_6_.refs_2_), channel_id=1, source_target_pairs={{0,8},{8,0},{16,24},{24,16},{1,9},{9,1},{17,25},{25,17},{2,10},{10... | collective-permute-start | bytes 393224 | tf_op jit(solution)/shard_map/ppermute | solution.py:476
  33.3 8.7 %collective-permute-start.21 = (f32[2,128,128]{2,1,0:T(8,128)S(1)}, f32[2,128,128]{2,1,0:T(8,128)S(1)}, u32[]{:S(2)}, u32[]{:S(2)}) collective-permute-start(f32[2,128,128]{2,1,0:T(8,128)S(1)} %pull.1.refs_6_.refs_2_), channel_id=1, source_target_pairs={{0,16},{8,24},{16,0},{24,8},{1,17},{9,25},{17,1},{25,9},{2,18},{10... | collective-permute-start | bytes 393224 | tf_op jit(solution)/shard_map/ppermute | solution.py:476
  34.2 7.8 %collective-permute-start.22 = (f32[2,128,128]{2,1,0:T(8,128)S(1)}, f32[2,128,128]{2,1,0:T(8,128)S(1)}, u32[]{:S(2)}, u32[]{:S(2)}) collective-permute-start(f32[2,128,128]{2,1,0:T(8,128)S(1)} %pull.1.refs_6_.refs_2_), channel_id=1, source_target_pairs={{0,24},{8,16},{16,8},{24,0},{1,25},{9,17},{17,9},{25,1},{2,26},{10... | collective-permute-start | bytes 393224 | tf_op jit(solution)/shard_map/ppermute | solution.py:476
  37.5 10.1 %collective-permute-start.17 = (f32[2,8,8,128]{3,2,1,0:T(8,128)S(1)}, f32[2,8,8,128]{3,2,1,0:T(8,128)S(1)}, u32[]{:S(2)}, u32[]{:S(2)}) collective-permute-start(f32[2,8,8,128]{3,2,1,0:T(8,128)S(1)} %get-tuple-element.70), channel_id=1, source_target_pairs={{0,2},{1,3},{2,0},{3,1},{4,6},{5,7},{6,4},{7,5},{8,10},{9,11},{10,... | collective-permute-start | bytes 196616 | tf_op jit(solution)/shard_map/ppermute | solution.py:476
  38.2 9.5 %collective-permute-start.18 = (f32[2,8,8,128]{3,2,1,0:T(8,128)S(1)}, f32[2,8,8,128]{3,2,1,0:T(8,128)S(1)}, u32[]{:S(2)}, u32[]{:S(2)}) collective-permute-start(f32[2,8,8,128]{3,2,1,0:T(8,128)S(1)} %get-tuple-element.71), channel_id=1, source_target_pairs={{0,4},{1,5},{2,6},{3,7},{4,0},{5,1},{6,2},{7,3},{8,12},{9,13},{10,... | collective-permute-start | bytes 196616 | tf_op jit(solution)/shard_map/ppermute | solution.py:476
  41.8 6.1 %collective-permute-start.19 = (f32[2,8,8,128]{3,2,1,0:T(8,128)S(1)}, f32[2,8,8,128]{3,2,1,0:T(8,128)S(1)}, u32[]{:S(2)}, u32[]{:S(2)}) collective-permute-start(f32[2,8,8,128]{3,2,1,0:T(8,128)S(1)} %get-tuple-element.72), channel_id=1, source_target_pairs={{0,6},{1,7},{2,4},{3,5},{4,2},{5,3},{6,0},{7,1},{8,14},{9,15},{10,... | collective-permute-start | bytes 196616 | tf_op jit(solution)/shard_map/ppermute | solution.py:476
